TPU v7x, 32 devices: a whole 2x2x4 slice. The times are simulated.
32 devices in a mesh: dp: 2 (over x), row: 4 (over y, core), col: 4 (over z).
Axes of the slice: x: 2, y: 2, z: 4, core: 2. Of those that a mesh axis runs over, the one named last changes fastest.
Arguments:
- residual_in: float32 [12288, 1280], P(('dp', 'row'), 'col'), may hold values from -6 to 6
- seq_ids: int32 [12288], P('dp'), may hold values from 0 to 3, as said below
- norm1_gain: float32 [1280], P('col'), may hold values from 0.1 to 1.9
- w_qkv: float32 [1280, 3, 1280], P('row', None, 'col'), may hold values from -0.15625 to 0.15625
- per_dim: float32 [80], replicated, may hold values from 0 to 1.5
- w_out: float32 [1280, 1280], P('col', 'row'), may hold values from -1.25 to 1.25
- norm2_gain: float32 [1280], P('col'), may hold values from 0.1 to 1.9
- w_up: float32 [1280, 1280], P('row', 'col'), may hold values from -0.15625 to 0.15625
- w_down: float32 [1280, 1280], P('col', 'row'), may hold values from -0.15625 to 0.15625
- out_grad: float32 [12288, 1280], P(('dp', 'row'), 'col'), may hold values from -6 to 6
Outputs:
- output: float32 [12288, 1280], P(('dp', 'row'), 'col')
- input_grad: float32 [12288, 1280], P(('dp', 'row'), 'col')
- norm1_gain_grad: float32 [1280], P('col')
- w_qkv_grad: float32 [1280, 3, 1280], P('row', None, 'col')
- per_dim_grad: float32 [80], replicated
- w_out_grad: float32 [1280, 1280], P('col', 'row')
- norm2_gain_grad: float32 [1280], P('col')
- w_up_grad: float32 [1280, 1280], P('row', 'col')
- w_down_grad: float32 [1280, 1280], P('col', 'row')
Inputs may be any that keep to these rules, and one draw needn't show every extreme that they name: seq_ids never fall; the 6144 tokens of one index g of dp hold exactly 2 sequences, numbered g * 2 to g * 2 + 1; each sequence starts at a multiple of 256 tokens within the group and has at least 768 tokens.
All inputs are finite; a program needn't handle non-finite values.
Results may differ from a plain program's by a relative error of at most 0.017.
The roundings to bfloat16 on the way count: a program that leaves them out, or rounds other values in their place, can miss the bound.
Values may be sent and summed in bfloat16 or wider, within the bound.
No kernel may reach another device: no remote copies, remote signals or barrier semaphores. Data moves between devices by JAX's collectives and lax.ppermute only.
A program may use at most 320 MiB of HBM per device.

v0:
```python
import functools
import math

import jax
import jax.numpy as jnp
from jax import lax
from jax.experimental import pallas as pl
from jax.experimental.pallas import tpu as pltpu
from jax.sharding import PartitionSpec as P

D = 1280
HD = 80
BLK = 256
LANES = 128

epsilon = 1e-06
scale_base = 1.442695041
excluded = -1e30

bf16 = jnp.bfloat16
f32 = jnp.float32


def dot(left, right):
    return jnp.dot(left, right, preferred_element_type=f32)


def product(form, left, right):
    return jnp.einsum(form, left, right, preferred_element_type=f32)


def three_terms(values):
    high = values.astype(bf16)
    rest = values - high.astype(f32)
    middle = rest.astype(bf16)
    return [high, middle, (rest - middle.astype(f32)).astype(bf16)]


def block_bias(starts_ref, first_block, width, block_count):
    shape = (block_count, width)
    block = lax.broadcasted_iota(jnp.int32, shape, 0)
    own = lax.broadcasted_iota(jnp.int32, shape, 1) // BLK
    start = jnp.zeros(shape, jnp.int32)
    for number in range(width // BLK):
        start = jnp.where(own == number, starts_ref[first_block + number], start)
    return jnp.where((block >= start) & (block <= first_block + own), 0.0, excluded).astype(bf16)


def extended(top, width, block_count, first_block, extra):
    row = lax.broadcasted_iota(jnp.int32, (LANES - HD, width), 0)
    block = first_block + lax.broadcasted_iota(jnp.int32, (LANES - HD, width), 1) // BLK
    marks = (row >= block_count) & (row < block_count + extra)
    if block_count:
        marks = marks | (row == block)
    return jnp.concatenate([top, jnp.where(marks, 1.0, 0.0).astype(bf16)], axis=0).T


def padded(parts, width):
    used = sum(part.shape[0] for part in parts)
    return jnp.concatenate(list(parts) + [jnp.zeros((LANES - used, width), bf16)], axis=0)


def store_pieces(ref, value, source, number, part):
    width, tile = ref.shape[2], value.shape[1]
    if width >= tile:
        ref[source * (part // width), :, pl.ds(pl.multiple_of(number * tile, tile), tile)] = value
        return
    first = source * (part // width) + number * (tile // width)
    for at in range(tile // width):
        ref[first + at] = value[:, at * width : (at + 1) * width]


def load_pieces(ref, source, number, part, tile):
    width = ref.shape[2]
    if width >= tile:
        return ref[source * (part // width), :, pl.ds(pl.multiple_of(number * tile, tile), tile)]
    grain = math.gcd(width, tile)
    chunks = []
    for at in range(tile // grain):
        start = number * tile + at * grain
        column = pl.multiple_of(lax.rem(start, width), grain)
        chunks.append(ref[source * (part // width) + start // width, :, pl.ds(column, grain)])
    return jnp.concatenate(chunks, axis=1)


def forward_kernel(starts_ref, place_ref, *refs, tokens, part, tile, rows):
    pieces = refs[: -5]
    out_ref, lse_ref, qkv_ref, leave_ref, key_scr = refs[-5:]
    half = pieces[0].shape[1]
    for number, piece in enumerate(pieces):
        flip, at = number % rows, number // rows
        qkv_ref[jnp.bitwise_xor(place_ref[0], flip), :, at * half : (at + 1) * half] = piece[...]
    block_count = tokens // BLK
    per_part = part // tile
    per_tile = tile // BLK
    for number in range(tokens // tile):
        source, at = divmod(number, per_part)
        key_scr[number * tile : (number + 1) * tile, :] = extended(
            qkv_ref[source, HD : 2 * HD, at * tile : (at + 1) * tile],
            tile,
            block_count,
            number * per_tile,
            0,
        )

    def query_tile(number, carried):
        source = number // per_part
        at = pl.multiple_of((number % per_part) * tile, tile)
        bias = block_bias(starts_ref, number * per_tile, tile, block_count)
        query = padded([qkv_ref[source, 0:HD, pl.ds(at, tile)], bias], tile)

        def key_tile(key_number, state):
            largest, total, result = state
            keys = key_scr[pl.ds(pl.multiple_of(key_number * tile, tile), tile), :]
            scores = dot(keys, query)
            key_at = pl.multiple_of((key_number % per_part) * tile, tile)
            values = qkv_ref[key_number // per_part, 2 * HD : 3 * HD, pl.ds(key_at, tile)]
            newest = jnp.maximum(largest, jnp.max(scores, axis=0, keepdims=True))
            factor = jnp.exp(largest - newest)
            weights = jnp.exp(scores - newest)
            total = total * factor + jnp.sum(weights, axis=0, keepdims=True)
            result = result * factor + dot(values, weights.astype(bf16))
            return newest, total, result

        largest, total, result = lax.fori_loop(
            starts_ref[number * per_tile] // per_tile,
            number + 1,
            key_tile,
            (
                jnp.full((1, tile), -jnp.inf, f32),
                jnp.zeros((1, tile), f32),
                jnp.zeros((HD, tile), f32),
            ),
        )
        result = result / total
        out_ref[source, :, pl.ds(at, tile)] = result
        store_pieces(leave_ref, result.astype(bf16), source, number % per_part, part)
        lse_ref[source, :, pl.ds(at, tile)] = largest + jnp.log(total)
        return carried

    lax.fori_loop(0, tokens // tile, query_tile, 0)


def backward_kernel(
    starts_ref,
    place_ref,
    scale_ref,
    qkv_ref,
    go_ref,
    out_ref,
    lse_ref,
    *refs,
    tokens,
    part,
    tile,
    rows,
):
    pieces = refs[: -6]
    dim_ref, grad_ref, key_scr, value_scr, key_grad, value_grad = refs[-6:]
    block_count = tokens // BLK
    per_part = part // tile
    per_tile = tile // BLK
    for number in range(tokens // tile):
        source, at = divmod(number, per_part)
        columns = slice(at * tile, (at + 1) * tile)
        band = slice(number * tile, (number + 1) * tile)
        key_scr[band, :] = extended(
            qkv_ref[source, HD : 2 * HD, columns], tile, block_count, number * per_tile, 3
        )
        value_scr[band, :] = extended(qkv_ref[source, 2 * HD : 3 * HD, columns], tile, 0, 0, 3)
    key_grad[...] = jnp.zeros_like(key_grad)
    value_grad[...] = jnp.zeros_like(value_grad)

    def query_tile(number, dim_total):
        source = number // per_part
        at = pl.multiple_of((number % per_part) * tile, tile)
        query_t = qkv_ref[source, 0:HD, pl.ds(at, tile)]
        go_t = load_pieces(go_ref, source, number % per_part, part, tile)
        delta = jnp.sum(
            go_t.astype(f32) * out_ref[source, :, pl.ds(at, tile)], axis=0, keepdims=True
        )
        lse = lse_ref[source, :, pl.ds(at, tile)]
        bias = block_bias(starts_ref, number * per_tile, tile, block_count)
        query_ext = padded([query_t, bias] + three_terms(-lse), tile)
        go_ext = padded([go_t] + three_terms(-delta), tile)
        query = padded([query_t], tile).T
        go = padded([go_t], tile).T

        def key_tile(key_number, total):
            band = pl.ds(pl.multiple_of(key_number * tile, tile), tile)
            key_at = pl.multiple_of((key_number % per_part) * tile, tile)
            keys_t = qkv_ref[key_number // per_part, HD : 2 * HD, pl.ds(key_at, tile)]
            weights = jnp.exp(dot(key_scr[band, :], query_ext))
            slopes = (weights * dot(value_scr[band, :], go_ext)).astype(bf16)
            value_grad[band, :] += dot(weights.astype(bf16), go)
            key_grad[band, :] += dot(slopes, query)
            return total + dot(keys_t, slopes)

        grad = lax.fori_loop(
            starts_ref[number * per_tile] // per_tile,
            number + 1,
            key_tile,
            jnp.zeros((HD, tile), f32),
        )
        grad_ref[source, 0:HD, pl.ds(at, tile)] = (grad * scale_ref[...]).astype(bf16)
        return dim_total + jnp.sum(grad * query_t.astype(f32), axis=1, keepdims=True)

    dim_ref[...] = lax.fori_loop(0, tokens // tile, query_tile, jnp.zeros((HD, 1), f32))
    for number in range(tokens // tile):
        source, at = divmod(number, per_part)
        columns = slice(at * tile, (at + 1) * tile)
        band = slice(number * tile, (number + 1) * tile)
        grad_ref[source, HD : 2 * HD, columns] = key_grad[band, :].T[:HD].astype(bf16)
        grad_ref[source, 2 * HD : 3 * HD, columns] = value_grad[band, :].T[:HD].astype(bf16)
    half = pieces[0].shape[1]
    for number, piece in enumerate(pieces):
        flip, at = number % rows, number // rows
        piece[...] = grad_ref[
            jnp.bitwise_xor(place_ref[0], flip), :, at * half : (at + 1) * half
        ]


in_vmem = pl.BlockSpec(memory_space=pltpu.VMEM)
in_smem = pl.BlockSpec(memory_space=pltpu.SMEM)


def attend(starts, place, pieces, rows, part, tile, width):
    tokens = rows * part
    return pl.pallas_call(
        functools.partial(forward_kernel, tokens=tokens, part=part, tile=tile, rows=rows),
        out_shape=(
            jax.ShapeDtypeStruct((rows, HD, part), f32),
            jax.ShapeDtypeStruct((rows, 1, part), f32),
            jax.ShapeDtypeStruct((rows, 3 * HD, part), bf16),
            jax.ShapeDtypeStruct((tokens // width, HD, width), bf16),
        ),
        in_specs=[in_smem] * 2 + [in_vmem] * len(pieces),
        out_specs=(in_vmem,) * 4,
        scratch_shapes=[pltpu.VMEM((tokens, LANES), bf16)],
        compiler_params=pltpu.CompilerParams(vmem_limit_bytes=60 << 20),
        cost_estimate=pl.CostEstimate(
            flops=3 * LANES * tokens * tokens,
            bytes_accessed=12 << 20,
            transcendentals=tokens * tokens // 3,
        ),
    )(starts, place, *pieces)


def attend_back(starts, place, scale, qkv, go, out, lse, tile, half):
    rows, _, part = qkv.shape
    tokens = rows * part
    count = rows * (part // half)
    results = pl.pallas_call(
        functools.partial(backward_kernel, tokens=tokens, part=part, tile=tile, rows=rows),
        out_shape=(jax.ShapeDtypeStruct((3 * HD, half), bf16),) * count
        + (jax.ShapeDtypeStruct((HD, 1), f32),),
        in_specs=[in_smem] * 2 + [in_vmem] * 5,
        out_specs=(in_vmem,) * (count + 1),
        scratch_shapes=[pltpu.VMEM((rows, 3 * HD, part), bf16)]
        + [pltpu.VMEM((tokens, LANES), bf16)] * 2
        + [pltpu.VMEM((tokens, LANES), f32)] * 2,
        compiler_params=pltpu.CompilerParams(vmem_limit_bytes=60 << 20),
        cost_estimate=pl.CostEstimate(
            flops=8 * LANES * tokens * tokens,
            bytes_accessed=16 << 20,
            transcendentals=tokens * tokens // 3,
        ),
    )(starts, place, scale.reshape(HD, 1), qkv, go, out, lse)
    return results[:-1], results[-1]


def assemble_kernel(here_ref, place_ref, group_ref, *refs, cols, splits):
    blocks, out_ref = refs[:-1], refs[-1]
    part = out_ref.shape[1] // len(blocks)
    width = out_ref.shape[2] // cols
    for number, block in enumerate(blocks):
        row = jnp.bitwise_xor(place_ref[0], number // splits)
        piece = jnp.bitwise_xor(group_ref[0], number % splits)
        band = pl.ds(pl.multiple_of((row * splits + piece) * part, 16), part)
        for col in range(cols):
            value = block[lax.rem(here_ref[0] + cols - col, cols), 0:part, :]
            for matrix in range(3):
                out_ref[matrix, band, col * width : (col + 1) * width] = value[
                    :, matrix * width : (matrix + 1) * width
                ]


def unrolled(count, body, value):
    for number in range(count):
        value = body(number, value)
    return value


def feed_kernel(
    here_ref,
    place_ref,
    att_ref,
    normed_ref,
    inverse_ref,
    gains_ref,
    w_hbm,
    *refs,
    rows,
    cols,
    heads,
    twins,
    order,
):
    go_pieces, change_pieces = refs[:cols], refs[cols : 2 * cols]
    back_ref, gain_ref, leave_ref, rhs_ref = refs[2 * cols : 2 * cols + 4]
    lhs_refs = refs[2 * cols + 4 : -12]
    (
        w_ref,
        attended,
        normed_two,
        branch_grad,
        go_ref,
        branch,
        middle,
        grad_two,
        flipped,
        flipped_go,
        grad_att,
        done,
    ) = refs[-12:]
    width, sub = go_pieces[0].shape
    copies = [
        pltpu.make_async_copy(w_hbm.at[number], w_ref.at[number], done.at[number])
        for number in range(3)
    ]
    for copy in copies:
        copy.start()

    def ring(shift):
        return pl.ds(pl.multiple_of(lax.rem(here_ref[0] + shift, cols) * width, 16), width)

    for number, piece in enumerate(go_pieces):
        go_ref[ring(cols - number), :] = piece[...]
    step = 256
    for col in range(cols):
        for head in range(heads):
            at = (col * heads + head) * HD
            attended[at : at + HD, :] = att_ref[head * twins * cols + col]
    inverse = inverse_ref[...]
    copies[0].wait()

    def part(number):
        return pl.ds(number * step, step)

    def first(number, total):
        at = part(number)
        here = dot(w_ref[0, at, :], attended[...])
        branch[at, :] = here
        mid = normed_ref[at, :].astype(f32) / (inverse * gains_ref[at, 0:1]) + here
        middle[at, :] = mid
        flipped_go[:, at] = go_ref[at, :].T
        rhs_ref[0, :, at] = attended[at, :].T
        return total + jnp.sum(mid * mid, axis=0, keepdims=True)

    steps = D // step
    total = unrolled(steps, first, jnp.zeros((1, sub), f32))
    inverse_two = lax.rsqrt(total / D + epsilon)
    copies[1].wait()
    copies[2].wait()

    def second(number, carried):
        at = part(number)
        value = (middle[at, :] * inverse_two * gains_ref[at, 1:2]).astype(bf16)
        normed_two[at, :] = value
        flipped[:, at] = value.T
        return carried

    unrolled(steps, second, 0)

    def third(number, carried):
        at = part(number)
        up_proj = dot(flipped[...], w_ref[1, :, at])
        sigmoid_up = jax.nn.sigmoid(up_proj)
        rhs_ref[2, :, at] = (up_proj * sigmoid_up).astype(bf16)
        grad_act = dot(flipped_go[...], w_ref[2, :, at])
        rhs_ref[1, :, at] = (
            grad_act * sigmoid_up * (1.0 + up_proj * (1.0 - sigmoid_up))
        ).astype(bf16)
        return carried

    unrolled(steps, third, 0)

    def fourth(number, along):
        at = part(number)
        branch[at, :] += dot_last(w_ref[2, at, :], rhs_ref[2])
        grad = dot_last(w_ref[1, at, :], rhs_ref[1])
        grad_two[at, :] = grad
        return along + jnp.sum(gains_ref[at, 1:2] * grad * middle[at, :], axis=0, keepdims=True)

    along = unrolled(steps, fourth, jnp.zeros((1, sub), f32))
    shrink = inverse_two * inverse_two * inverse_two * along / D

    def fifth(number, carried):
        at = part(number)
        grad = grad_two[at, :]
        mid = middle[at, :]
        back = inverse_two * gains_ref[at, 1:2] * grad - mid * shrink
        back_ref[at, :] = (back / (inverse * gains_ref[at, 0:1])).astype(bf16)
        gain_ref[at, :] = jnp.sum(grad * mid * inverse_two, axis=1, keepdims=True)
        value = (go_ref[at, :].astype(f32) + back).astype(bf16)
        branch_grad[at, :] = value
        flipped[:, at] = value.T
        return carried

    unrolled(steps, fifth, 0)

    def sixth(number, carried):
        at = part(number)
        grad_att[at, :] = dot(flipped[...], w_ref[0, :, at]).T.astype(bf16)
        return carried

    unrolled(steps, sixth, 0)
    for number, piece in enumerate(change_pieces):
        piece[...] = branch[ring(number), :].astype(bf16)
    share = D // rows
    for slot, (out, at) in enumerate(order):
        row = jnp.bitwise_xor(place_ref[0], slot) if len(lhs_refs) > 1 else slot
        band = pl.ds(pl.multiple_of(row * share, 16), share)
        for number, value in enumerate((branch_grad, normed_two, go_ref)):
            lhs_refs[out][at, number] = value[band, :]
    for row in range(rows):
        for col in range(cols):
            at = (col * heads + row // twins) * HD
            leave_ref[row * cols + col] = grad_att[at : at + HD, :]


def dot_last(left, right):
    return lax.dot_general(left, right, (((1,), (1,)), ((), ())), preferred_element_type=f32)


def weights_kernel(here_ref, group_ref, *refs, count, splits):
    operands, outs = refs[:count], refs[count:]
    cols, part, wide = outs[0].shape
    width = wide // 3
    for index, out in enumerate(outs):
        slot = index // splits
        piece = jnp.bitwise_xor(group_ref[0], index % splits)
        band = pl.ds(pl.multiple_of(piece * part, 16), part)
        for number in range(3):
            value = sum(
                dot(operands[at][slot, number, band, :], operands[at + 1][number])
                for at in range(0, count, 2)
            ).astype(bf16)
            for col in range(cols):
                place = lax.rem(col + cols - here_ref[0], cols)
                out[place, :, number * width : (number + 1) * width] = value[
                    :, col * width : (col + 1) * width
                ]


def assemble(here, place, group, blocks, splits):
    cols = blocks[0].shape[0]
    return pl.pallas_call(
        functools.partial(assemble_kernel, cols=cols, splits=splits),
        out_shape=jax.ShapeDtypeStruct((3, D, D), bf16),
        in_specs=[in_smem] * 3 + [in_vmem] * len(blocks),
        out_specs=in_vmem,
        compiler_params=pltpu.CompilerParams(vmem_limit_bytes=60 << 20),
        cost_estimate=pl.CostEstimate(flops=0, bytes_accessed=20 << 20, transcendentals=0),
    )(here, place, group, *blocks)


def feed_forward(
    here, place, attended, pieces, normed, inverse, gains, weights, rows, cols, heads, twins, shapes, order
):
    width, sub = pieces[0].shape
    results = pl.pallas_call(
        functools.partial(
            feed_kernel, rows=rows, cols=cols, heads=heads, twins=twins, order=order
        ),
        out_shape=(jax.ShapeDtypeStruct((width, sub), bf16),) * cols
        + (
            jax.ShapeDtypeStruct((D, sub), bf16),
            jax.ShapeDtypeStruct((D, 1), f32),
            jax.ShapeDtypeStruct((rows * cols, HD, sub), bf16),
            jax.ShapeDtypeStruct((3, sub, D), bf16),
        )
        + tuple(jax.ShapeDtypeStruct(shape, bf16) for shape in shapes),
        in_specs=[in_smem] * 2
        + [in_vmem] * 4
        + [pl.BlockSpec(memory_space=pl.ANY)]
        + [in_vmem] * cols,
        out_specs=(in_vmem,) * (cols + 4 + len(shapes)),
        scratch_shapes=[pltpu.VMEM((3, D, D), bf16)]
        + [pltpu.VMEM((D, sub), bf16)] * 4
        + [pltpu.VMEM((D, sub), f32)] * 3
        + [pltpu.VMEM((sub, D), bf16)] * 2
        + [pltpu.VMEM((D, sub), bf16), pltpu.SemaphoreType.DMA((3,))],
        compiler_params=pltpu.CompilerParams(vmem_limit_bytes=60 << 20),
        cost_estimate=pl.CostEstimate(
            flops=12 * D * D * sub, bytes_accessed=20 << 20, transcendentals=D * sub
        ),
    )(here, place, attended, normed, inverse, gains, weights, *pieces)
    return results[:cols], results[cols : cols + 4], results[cols + 4 :]


def weight_grads(here, group, pairs, cols, splits):
    slots, _, share, sub = pairs[0].shape
    count = slots * splits
    return pl.pallas_call(
        functools.partial(weights_kernel, count=len(pairs), splits=splits),
        out_shape=(jax.ShapeDtypeStruct((cols, share // splits, 3 * D // cols), bf16),) * count,
        in_specs=[in_smem] * 2 + [in_vmem] * len(pairs),
        out_specs=(in_vmem,) * count,
        compiler_params=pltpu.CompilerParams(vmem_limit_bytes=60 << 20),
        cost_estimate=pl.CostEstimate(
            flops=6 * D * D * sub, bytes_accessed=16 << 20, transcendentals=0
        ),
    )(here, group, *pairs)


def copies_kernel(place_ref, *refs):
    blocks, (whole, turned) = refs[:-2], refs[-2:]
    share = blocks[0].shape[0]
    for flip, block in enumerate(blocks):
        row = jnp.bitwise_xor(place_ref[0], flip)
        whole[pl.ds(pl.multiple_of(row * share, 16), share), :] = block[...]
    for number in range(D // LANES):
        at = slice(number * LANES, (number + 1) * LANES)
        turned[:, at] = whole[at, :].T


def projection_copies(place, blocks):
    share, wide = blocks[0].shape
    return pl.pallas_call(
        copies_kernel,
        out_shape=(
            jax.ShapeDtypeStruct((D, wide), bf16),
            jax.ShapeDtypeStruct((wide, D), bf16),
        ),
        in_specs=[in_smem] + [in_vmem] * len(blocks),
        out_specs=(in_vmem,) * 2,
        compiler_params=pltpu.CompilerParams(vmem_limit_bytes=60 << 20),
        cost_estimate=pl.CostEstimate(flops=0, bytes_accessed=8 << 20, transcendentals=0),
    )(place, *blocks)


def project_kernel(place_ref, turned_ref, factor_ref, normed_ref, *refs, rows, heads):
    outs, result = refs[:-1], refs[-1]
    for head in range(heads):
        at = slice(head * 3 * HD, (head + 1) * 3 * HD)
        value = dot(turned_ref[at, :], normed_ref[...]) * factor_ref[at, :]
        result[head] = value.astype(bf16)
    for flip, out in enumerate(outs):
        out[...] = result[jnp.bitwise_xor(place_ref[0], flip) // (rows // heads)]


def project(place, turned, factors, normed, rows, heads):
    half = normed.shape[1]
    return pl.pallas_call(
        functools.partial(project_kernel, rows=rows, heads=heads),
        out_shape=(jax.ShapeDtypeStruct((3 * HD, half), bf16),) * rows,
        in_specs=[in_smem] + [in_vmem] * 3,
        out_specs=(in_vmem,) * rows,
        scratch_shapes=[pltpu.VMEM((heads, 3 * HD, half), bf16)],
        compiler_params=pltpu.CompilerParams(vmem_limit_bytes=60 << 20),
        cost_estimate=pl.CostEstimate(
            flops=2 * D * turned.shape[0] * half, bytes_accessed=10 << 20, transcendentals=0
        ),
    )(place, turned, factors, normed)


def back_kernel(here_ref, place_ref, whole_ref, *refs, rows, cols, heads):
    normed, back_ref, pieces, (payload, grads) = refs[:2], refs[2], refs[3:-2], refs[-2:]
    half = normed[0].shape[1]
    width = D // cols
    sub = back_ref.shape[1]
    here = here_ref[0]
    gather_heads(place_ref, pieces, grads, heads)
    for number in range(2):
        along = jnp.zeros((1, half), f32)
        tokens = slice(number * half, (number + 1) * half)
        for col in range(cols):
            at = slice(col * width, (col + 1) * width)
            value = dot(whole_ref[at, :], grads[:, tokens])
            along += jnp.sum(value * normed[number][at, :].astype(f32), axis=0, keepdims=True)
            for quarter in range(half // sub):
                columns = slice(quarter * sub, (quarter + 1) * sub)
                into = slice(number * half + quarter * sub, number * half + (quarter + 1) * sub)
                mine = jnp.where(here == number * (half // sub) + quarter, 1.0, 0.0)
                payload[col, 0:width, into] = (
                    value[:, columns] + back_ref[at, :].astype(f32) * mine
                ).astype(bf16)
        tail = jnp.concatenate([along, jnp.zeros((15, half), f32)], axis=0).astype(bf16)
        for col in range(cols):
            payload[col, width : width + 16, tokens] = tail


def gather_heads(place_ref, pieces, grads, heads):
    for flip, piece in enumerate(pieces):
        head = jnp.bitwise_xor(place_ref[0], flip) // (len(pieces) // heads)
        grads[pl.ds(pl.multiple_of(head * 3 * HD, 16), 3 * HD), :] = piece[...]


def project_back(here, place, whole, normed, back, pieces, rows, cols, heads):
    count = 2 * normed[0].shape[1]
    width = D // cols
    return pl.pallas_call(
        functools.partial(back_kernel, rows=rows, cols=cols, heads=heads),
        out_shape=jax.ShapeDtypeStruct((cols, width + 16, count), bf16),
        in_specs=[in_smem] * 2 + [in_vmem] * (4 + rows),
        out_specs=in_vmem,
        scratch_shapes=[pltpu.VMEM((3 * width, count), bf16)],
        compiler_params=pltpu.CompilerParams(vmem_limit_bytes=60 << 20),
        cost_estimate=pl.CostEstimate(
            flops=2 * D * 3 * width * count, bytes_accessed=16 << 20, transcendentals=0
        ),
    )(here, place, whole, *normed, back, *pieces)


def projection_grads_kernel(place_ref, whole_ref, *refs, order, heads):
    outs, (gain_ref, grads) = refs[-2 - (1 + max(out for out, _ in order)) : -2], refs[-2:]
    normed, pieces = refs[:2], refs[2 : -2 - len(outs)]
    half = normed[0].shape[1]
    gather_heads(place_ref, pieces, grads, heads)
    share = outs[0].shape[1]
    for slot, (out, at) in enumerate(order):
        row = jnp.bitwise_xor(place_ref[0], slot) if len(outs) > 1 else slot
        band = pl.ds(pl.multiple_of(row * share, 16), share)
        value = dot_last(normed[0][band, :], grads[:, :half]) + dot_last(
            normed[1][band, :], grads[:, half:]
        )
        gain_ref[band, :] = jnp.sum(value * whole_ref[band, :].astype(f32), axis=1, keepdims=True)
        outs[out][at] = value.astype(bf16)


def projection_grads(place, whole, normed, pieces, heads, shapes, order):
    half = normed[0].shape[1]
    return pl.pallas_call(
        functools.partial(projection_grads_kernel, order=order, heads=heads),
        out_shape=tuple(jax.ShapeDtypeStruct(shape, bf16) for shape in shapes)
        + (jax.ShapeDtypeStruct((D, 1), f32),),
        in_specs=[in_smem] + [in_vmem] * (3 + len(pieces)),
        out_specs=(in_vmem,) * (len(shapes) + 1),
        scratch_shapes=[pltpu.VMEM((whole.shape[1], 2 * half), bf16)],
        compiler_params=pltpu.CompilerParams(vmem_limit_bytes=60 << 20),
        cost_estimate=pl.CostEstimate(
            flops=4 * D * whole.shape[1] * half, bytes_accessed=12 << 20, transcendentals=0
        ),
    )(place, whole, *normed, *pieces)


def after(values, *others):
    return lax.optimization_barrier((values,) + others)[0]


def partner(values, flip, size, axis="row"):
    return lax.ppermute(values, axis, [(at, at ^ flip) for at in range(size)])


def plane(values, splits):
    result = [values[0]]
    for index in range(1, len(values)):
        flip, other = index // splits * 2, index % splits
        result.append(
            lax.ppermute(
                values[index],
                ("dp", "row"),
                [(at, at ^ (other * 4 + flip)) for at in range(splits * 4)],
            )
            if splits == 2
            else partner(values[index], flip, 4)
        )
    return result


def swapped(pieces, rows):
    return [pieces[0]] + [partner(pieces[flip], flip, rows) for flip in range(1, rows)]


def spread_rows(values, rows):
    if rows != 4:
        return swapped([values] * rows, rows)
    far = partner(values, 2, rows)
    return [values, partner(values, 1, rows), far, partner(far, 1, rows)]


def add(left, right):
    return left.astype(f32) + right.astype(f32)


def total(values, axes):
    for axis, size in axes:
        flip = 1
        while flip < size:
            values = values + partner(values, flip, size, axis)
            flip *= 2
    return values


def sum_groups(values, groups):
    if groups == 2:
        return add(values, partner(values, 1, 2, "dp"))
    return lax.psum(values, "dp").astype(f32)


def ring_swap(pieces, cols):
    return [pieces[0]] + [
        lax.ppermute(pieces[shift], "col", [(at, (at + shift) % cols) for at in range(cols)])
        for shift in range(1, cols)
    ]


def on_device(
    groups, rows, cols, residual_in, seq_ids, norm1_gain, w_qkv, per_dim, w_out, norm2_gain, w_up, w_down, out_grad
):
    count, width = residual_in.shape
    heads = width // HD
    twins = rows // heads
    sub = count // cols
    half = count // 2
    share = w_qkv.shape[0]
    tile = 768 if count % 768 == 0 else BLK
    back_tile = 512 if count % 512 == 0 else tile
    here = lax.axis_index("col")
    place = lax.axis_index("row")
    here_of, place_of = here[None].astype(jnp.int32), place[None].astype(jnp.int32)

    block_seq = seq_ids[::BLK]
    starts = jnp.sum((block_seq[None, :] < block_seq[:, None]).astype(jnp.int32), axis=1)

    residual = residual_in.T
    squares = jnp.sum(residual * residual, axis=0)
    squares = squares + partner(squares, 1, cols, "col")
    inverse_one = lax.rsqrt((squares + partner(squares, 2, cols, "col")) / D + epsilon)[None, :]
    normed = (residual * inverse_one * norm1_gain[:, None]).astype(bf16)
    qkv_local = w_qkv.astype(bf16).reshape(share, 3, heads, HD).transpose(0, 2, 1, 3)
    qkv_local = qkv_local.reshape(share, heads * 3 * HD)
    whole, turned = projection_copies(place_of, spread_rows(qkv_local, rows))
    scale = jax.nn.softplus(per_dim) * scale_base / math.sqrt(HD)
    factors = jnp.tile(jnp.concatenate([scale, jnp.ones((2 * HD,), f32)]), heads)[:, None]
    stacked = jnp.concatenate(
        [w_out.T, w_up, w_down.T], axis=1
    ).astype(bf16)
    gains = [jnp.concatenate(three_terms(gain))[None] for gain in (norm1_gain, norm2_gain)]
    splits = 2 if groups == 2 and rows == 4 else 1
    part = share // splits
    group_of = jnp.zeros((1,), jnp.int32)
    if splits == 2:
        group = lax.axis_index("dp")
        group_of = group[None].astype(jnp.int32)
        stacked = lax.dynamic_slice_in_dim(stacked, group * part, part, 0)
    stacked = jnp.concatenate([stacked] + gains + [jnp.zeros((14, 3 * width), bf16)], axis=0)
    gathered = jnp.stack(ring_swap([after(stacked, turned)] * cols, cols))
    gains = gathered[:, part : part + 2].astype(f32).reshape(cols, 2, 3, width).sum(axis=2)
    gains = jnp.concatenate(
        [
            lax.dynamic_index_in_dim(gains, lax.rem(here + cols - col, cols), 0, keepdims=False)
            for col in range(cols)
        ],
        axis=1,
    ).T
    near = [gathered]
    if rows == 4:
        if splits == 2:
            near.append(partner(gathered, 1, 2, "dp"))
        near.append(partner(gathered, 2, rows))
        if splits == 2:
            near.append(partner(after(near[2], near[1]), 1, 2, "dp"))

    out_grad_t = out_grad.T.astype(bf16)

    def quarter(values, shift):
        at = lax.rem(here + shift, cols) * sub
        return lax.dynamic_slice_in_dim(values, at, sub, 1)

    grad_pieces = [quarter(out_grad_t, shift) for shift in range(cols)]

    pieces, normed_parts = [], []
    for at in range(2):
        part = normed[:, at * half : (at + 1) * half]
        if at:
            part = after(part, turned, *grad_pieces)
        normed_parts.append(lax.all_gather(part, "col", axis=0, tiled=True))
        outs = project(place_of, turned, factors, normed_parts[at], rows, heads)
        pieces += swapped(outs, rows)

    tidy = sub % LANES == 0
    if rows == 4:
        pieces[0] = after(pieces[0], *near[1:3])
    result, lse, qkv_heads, leaving = attend(
        starts, place_of, pieces, rows, count, tile, sub if tidy else count
    )
    if rows == 4:
        near = [after(value, lse) for value in near]
        other = [partner(value, 1, rows) for value in near]
        blocks = near[:splits] + other[:splits] + near[splits:] + other[splits:]
    else:
        blocks = spread_rows(gathered, rows)
    weights = assemble(here_of, place_of, group_of, blocks, splits)
    grad_pieces = ring_swap(grad_pieces, cols)

    if not tidy:
        leaving = leaving.reshape(rows, HD, cols, sub).transpose(0, 2, 1, 3)
        leaving = leaving.reshape(rows * cols, HD, sub)
    leaving = after(leaving, *grad_pieces)
    arrived = lax.all_to_all(leaving, ("row", "col"), 0, 0, tiled=True)

    own_inverse = quarter(inverse_one, 0)
    own_at = lax.rem(here, cols // 2) * sub
    own_normed = jnp.where(
        here < cols // 2,
        lax.dynamic_slice_in_dim(normed_parts[0], own_at, sub, 1),
        lax.dynamic_slice_in_dim(normed_parts[1], own_at, sub, 1),
    )
    wide = (share, 3 * width)
    pairwise = ((0, 0), (1, 0), (0, 1), (1, 1))
    natural = tuple((0, row) for row in range(rows))
    order, slots = (pairwise, 2) if rows == 4 else (natural, rows)
    change, (back_two, gain_two_part, leaving, rhs), lhs = feed_forward(
        here_of,
        place_of,
        arrived,
        grad_pieces,
        own_normed,
        own_inverse,
        gains,
        weights,
        rows,
        cols,
        heads,
        twins,
        ((slots, 3, share, sub),) * (rows // slots),
        order,
    )

    go = lax.all_to_all(leaving, ("row", "col"), 0, 0, tiled=True)
    if not tidy:
        go = go.reshape(rows, cols, HD, sub).transpose(0, 2, 1, 3).reshape(rows, HD, count)

    if rows == 4:
        pairs = [lhs[0], rhs, partner(lhs[1], 1, rows), partner(rhs, 1, rows)]
        mine = weight_grads(here_of, group_of, pairs, cols, splits)
        go = after(go, *mine)
        mine = plane(mine, splits)
    else:
        mine = jnp.stack(weight_grads(here_of, group_of, [lhs[0], rhs], cols, 1))
        mine = lax.psum_scatter(mine, "row", scatter_dimension=0, tiled=False)

    pieces, dim_part = attend_back(
        starts, place_of, scale, qkv_heads, go, result, lse, back_tile, count
    )
    arrived = swapped(pieces, rows)

    if rows == 4:
        mine = sum(after(value, arrived[1]).astype(f32) for value in mine).astype(bf16)
    mine = ring_swap([mine[shift] for shift in range(cols)], cols)
    mine = sum(value.astype(f32) for value in mine).astype(bf16)
    if splits == 2:
        mine = jnp.stack([mine, partner(mine, 1, 2, "dp")])
        shard = jnp.where(group == 0, mine, mine[::-1]).reshape(wide).astype(f32)
    else:
        shard = sum_groups(mine, groups)

    arrived[0] = after(arrived[0], mine)
    payload = project_back(
        here_of, place_of, whole, normed_parts, back_two, arrived, rows, cols, heads
    )
    summed = lax.psum_scatter(payload, "col", scatter_dimension=0, tiled=False).astype(f32)

    own_head = (place % twins == 0).astype(f32)
    *parts, gain_one_part = projection_grads(
        place_of,
        after(whole, payload),
        normed_parts,
        arrived,
        heads,
        ((slots,) + wide,) * (rows // slots),
        order,
    )
    small = jnp.concatenate([gain_one_part, gain_two_part, dim_part * own_head])[:, 0]
    if rows == 4:
        kept, sent = parts
        arrived = partner(sent, 1, rows)
        far = partner(add(kept[1], arrived[1]).astype(bf16), 2, rows)
        mine = (add(kept[0], arrived[0]) + far.astype(f32)).astype(bf16)
    else:
        mine = lax.psum_scatter(parts[0], "row", scatter_dimension=0, tiled=False)
    qkv_grad = sum_groups(mine, groups)
    qkv_grad = qkv_grad.reshape(share, heads, 3, HD).transpose(0, 2, 1, 3).reshape(share, 3, width)
    small = total(small, (("row", rows), ("dp", groups), ("col", cols)))
    gain_one_grad = lax.dynamic_slice_in_dim(small[:D], here * width, width) / norm1_gain
    gain_two_grad = lax.dynamic_slice_in_dim(small[D : 2 * D], here * width, width)
    scale_grad = small[2 * D :] / scale * (scale_base / math.sqrt(HD)) * jax.nn.sigmoid(per_dim)

    change = ring_swap(
        [after(piece, go if at % 2 else payload) for at, piece in enumerate(change)], cols
    )
    output = jnp.zeros_like(residual_in)
    for shift, piece in enumerate(change):
        at = lax.rem(here + cols - shift, cols) * sub
        piece = lax.dynamic_slice_in_dim(residual_in, at, sub, 0) + piece.astype(f32).T
        output = lax.dynamic_update_slice_in_dim(output, piece, at, 0)

    grad_one, along_one = summed[:width], summed[width : width + 1]
    back_one = inverse_one * norm1_gain[:, None] * grad_one - residual * inverse_one**2 * (
        along_one / D
    )
    input_grad = out_grad + back_one.T
    return (
        output,
        input_grad,
        gain_one_grad,
        qkv_grad,
        scale_grad,
        shard[:, :width].T,
        gain_two_grad,
        shard[:, width : 2 * width],
        shard[:, 2 * width :].T,
    )


def solution(mesh):
    in_specs = (
        P(("dp", "row"), "col"),
        P("dp"),
        P("col"),
        P("row", None, "col"),
        P(),
        P("col", "row"),
        P("col"),
        P("row", "col"),
        P("col", "row"),
        P(("dp", "row"), "col"),
    )
    out_specs = (
        P(("dp", "row"), "col"),
        P(("dp", "row"), "col"),
        P("col"),
        P("row", None, "col"),
        P(),
        P("col", "row"),
        P("col"),
        P("row", "col"),
        P("col", "row"),
    )
    return jax.shard_map(
        functools.partial(on_device, mesh.shape["dp"], mesh.shape["row"], mesh.shape["col"]),
        mesh=mesh,
        in_specs=in_specs,
        out_specs=out_specs,
        check_vma=False,
    )
```

profile of v0, /device:TPU:9, one launch (start us, length us, event | category | flops | bytes accessed | tf_op | source)
XLA Modules:
  0.0 492.6 jit_solution(18429792715879471315)
XLA Ops:
  7.2 1.8 multiply_reduce_fusion
  9.2 2.5 collective-permute-done.3
  11.7 2.3 collective-permute-start.4
  16.4 1.7 copy.60
  19.3 1.2 collective-permute-start.1
  20.5 3.3 collective-permute-start
  23.8 9.1 %collective-permute-done.1.refs_2_ = bf16[320,960]{1,0:T(8,128)(2,1)} collective-permute-done((bf16[320,960]{1,0:T(8,128)(2,1)}, bf16[320,960]{1,0:T(8,128)(2,1)}, u32[]{:S(2)}, u32[]{:S(2)}) %collective-permute-start.1) | collective-permute-done | bytes 614432 | tf_op jit(solution)/shard_map/ppermute | solution.py:653
  32.9 3.9 collective-permute-start.2
  36.8 1.6 convert_element_type.144
  39.5 4.2 shard_map.169
  45.8 2.4 collective-permute-start.6
  48.3 1.3 collective-permute-start.5
  49.6 33.7 %collective-permute-done.6 = bf16[176,960]{1,0:T(8,128)(2,1)S(1)} collective-permute-done((bf16[176,960]{1,0:T(8,128)(2,1)S(1)}, bf16[176,960]{1,0:T(8,128)(2,1)S(1)}, u32[]{:S(2)}, u32[]{:S(2)}) %collective-permute-start.6) | collective-permute-done | bytes 337952 | tf_op jit(solution)/shard_map/ppermute | solution.py:704
  83.4 9.9 %collective-permute-done.7 = bf16[176,960]{1,0:T(8,128)(2,1)S(1)} collective-permute-done((bf16[176,960]{1,0:T(8,128)(2,1)S(1)}, bf16[176,960]{1,0:T(8,128)(2,1)S(1)}, u32[]{:S(2)}, u32[]{:S(2)}) %collective-permute-start.7) | collective-permute-done | bytes 337952 | tf_op jit(solution)/shard_map/ppermute | solution.py:704
  97.0 5.7 %shard_map.170 = (bf16[240,768]{1,0:T(8,128)(2,1)}, bf16[240,768]{1,0:T(8,128)(2,1)}, bf16[240,768]{1,0:T(8,128)(2,1)}, bf16[240,768]{1,0:T(8,128)(2,1)}) custom-call(s32[1]{0:T(128)} %bitcast.1.place_ref, bf16[960,1280]{1,0:T(8,128)(2,1)} %get-tuple-element.65.turned_ref, f32[960,1]{1,0:T(8,128)} %broadcast_in_dim_tile.4.factor_ref, ...), custom_call_target="tpu_custom_call" | custom-call | flops 1887436800 | bytes 10485760 | tf_op jit(solution)/shard_map/pallas_call | solution.py:555
  104.0 1.4 collective-permute-start.12
  105.3 22.8 %all-gather.5.cloned.1.call-done.normed_ref.refs_1_ = bf16[1280,768]{1,0:T(8,128)(2,1)} async-done(((bf16[320,768]{1,0:T(8,128)(2,1)}), bf16[1280,768]{1,0:T(8,128)(2,1)}) %all-gather.5.cloned.1.call-update) | async-done | bytes 1966096 | tf_op jit(solution)/shard_map/all_gather | solution.py:779
  128.1 5.7 %shard_map.171 = (bf16[240,768]{1,0:T(8,128)(2,1)}, bf16[240,768]{1,0:T(8,128)(2,1)}, bf16[240,768]{1,0:T(8,128)(2,1)}, bf16[240,768]{1,0:T(8,128)(2,1)}) custom-call(s32[1]{0:T(128)} %bitcast.1.place_ref, bf16[960,1280]{1,0:T(8,128)(2,1)} %get-tuple-element.65.turned_ref, f32[960,1]{1,0:T(8,128)} %broadcast_in_dim_tile.4.factor_ref, ...), custom_call_target="tpu_custom_call" | custom-call | flops 1887436800 | bytes 10485760 | tf_op jit(solution)/shard_map/pallas_call | solution.py:555
  138.0 1.4 collective-permute-start.16
  139.3 6.2 %collective-permute-done.12.refs_3_ = bf16[240,768]{1,0:T(8,128)(2,1)} collective-permute-done((bf16[240,768]{1,0:T(8,128)(2,1)}, bf16[240,768]{1,0:T(8,128)(2,1)}, u32[]{:S(2)}, u32[]{:S(2)}) %collective-permute-start.12) | collective-permute-done | bytes 368672 | tf_op jit(solution)/shard_map/ppermute | solution.py:653
  146.7 4.3 collective-permute-done.14.refs_6_
  151.3 8.8 %collective-permute-done.15.refs_7_ = bf16[240,768]{1,0:T(8,128)(2,1)} collective-permute-done((bf16[240,768]{1,0:T(8,128)(2,1)}, bf16[240,768]{1,0:T(8,128)(2,1)}, u32[]{:S(2)}, u32[]{:S(2)}) %collective-permute-start.15) | collective-permute-done | bytes 368672 | tf_op jit(solution)/shard_map/ppermute | solution.py:653
  160.1 38.4 %shard_map.172 = (f32[4,80,1536]{2,1,0:T(8,128)}, f32[4,1,1536]{2,1,0:T(1,128)}, bf16[4,240,1536]{2,1,0:T(8,128)(2,1)}, bf16[16,80,384]{2,1,0:T(8,128)(2,1)}) custom-call(s32[24]{0:T(128)} %convert_reduce_fusion.starts_ref, s32[1]{0:T(128)} %bitcast.1.place_ref, bf16[240,768]{1,0:T(8,128)(2,1)} %get-tuple-element.68.refs_0_, ...), custom_call_target="tpu_custom_call" | custom-call | flops 14495514624 | bytes 12582912 | tf_op jit(solution)/shard_map/pallas_call | solution.py:229
  198.5 4.4 all-to-all-start
  206.1 2.7 dynamic-slice_select_fusion.normed_ref
  208.8 1.9 collective-permute-done.22.refs_6_
  210.7 2.1 collective-permute-done.20.refs_3_
  212.7 10.5 %shard_map.173.w_hbm = bf16[3,1280,1280]{2,1,0:T(8,128)(2,1)} custom-call(s32[1]{0:T(128)} %bitcast.here_ref, s32[1]{0:T(128)} %bitcast.1.place_ref, s32[1]{0:T(128)} %bitcast.21.group_ref, bf16[4,176,960]{2,1,0:T(8,128)(2,1)} %copy-done.2, bf16[4,176,960]{2,1,0:T(8,128)(2,1)} %collective-permute-done.8.refs_1_, ...), custom_call_target="tpu_custom_call" | custom-call | bytes 20971520 | tf_op jit(solution)/shard_map/pallas_call | solution.py:458
  223.2 1.5 all-to-all-done.att_ref
  224.8 17.6 %shard_map.174 = (bf16[320,384]{1,0:T(8,128)(2,1)}, bf16[320,384]{1,0:T(8,128)(2,1)}, bf16[320,384]{1,0:T(8,128)(2,1)}, bf16[320,384]{1,0:T(8,128)(2,1)}, bf16[1...) custom-call(s32[1]{0:T(128)} %bitcast.here_ref, ...), custom_call_target="tpu_custom_call" | custom-call | flops 7549747200 | bytes 20971520 | tf_op jit(solution)/shard_map/pallas_call | solution.py:472
  243.6 5.8 %all-to-all-start.1 = ((bf16[16,80,384]{2,1,0:T(8,128)(2,1)}), bf16[16,80,384]{2,1,0:T(8,128)(2,1)S(1)}, u32[]{:S(2)}, u32[]{:S(2)}) async-start(bf16[16,80,384]{2,1,0:T(8,128)(2,1)} %get-tuple-element.89), calls=%async_computation.1 | async-start | bytes 1966080 | tf_op jit(solution)/shard_map/all_to_all | solution.py:832
  250.6 2.5 collective-permute-done.24.refs_2_
  253.1 10.2 %shard_map.175 = (bf16[4,160,960]{2,1,0:T(8,128)(2,1)}, bf16[4,160,960]{2,1,0:T(8,128)(2,1)}, bf16[4,160,960]{2,1,0:T(8,128)(2,1)}, bf16[4,160,960]{2,1,0:T(8,128)(2,1)}) custom-call(s32[1]{0:T(128)} %bitcast.here_ref, s32[1]{0:T(128)} %bitcast.21.group_ref, bf16[2,3,320,384]{3,2,1,0:T(8,128)(2,1)} %get-tuple-element.90.refs_0_, ...), custom_call_target="tpu_custom_call" | custom-call | flops 3774873600 | bytes 16777216 | tf_op jit(solution)/shard_map/pallas_call | solution.py:505
  264.6 1.4 collective-permute-start.29
  266.0 5.7 %all-to-all-done.1.go_ref = bf16[16,80,384]{2,1,0:T(8,128)(2,1)S(1)} async-done(((bf16[16,80,384]{2,1,0:T(8,128)(2,1)}), bf16[16,80,384]{2,1,0:T(8,128)(2,1)S(1)}, u32[]{:S(2)}, u32[]{:S(2)}) %all-to-all-start.1) | async-done | bytes 983072 | tf_op jit(solution)/shard_map/all_to_all | solution.py:832
  272.6 54.1 %shard_map.176 = (bf16[240,1536]{1,0:T(8,128)(2,1)}, bf16[240,1536]{1,0:T(8,128)(2,1)}, bf16[240,1536]{1,0:T(8,128)(2,1)}, bf16[240,1536]{1,0:T(8,128)(2,1)}, f32[80,1]{1,0:T(8,128)}) custom-call(s32[24]{0:T(128)} %convert_reduce_fusion.starts_ref, s32[1]{0:T(128)} %bitcast.1.place_ref, f32[80,1]{1,0:T(8,128)} %copy.70.scale_ref, ...), custom_call_target="tpu_custom_call" | custom-call | flops 38654705664 | bytes 16777216 | tf_op jit(solution)/shard_map/pallas_call | solution.py:253
  327.7 2.1 collective-permute-done.26.refs_4_.refs_3_
  329.8 3.5 add_convert_fusion
  334.0 4.1 collective-permute-start.31
  339.0 2.1 collective-permute-start.35
  341.1 2.7 collective-permute-done.30
  343.8 18.3 %collective-permute-done.31 = bf16[160,960]{1,0:T(8,128)(2,1)S(1)} collective-permute-done((bf16[160,960]{1,0:T(8,128)(2,1)S(1)}, bf16[160,960]{1,0:T(8,128)(2,1)S(1)}, u32[]{:S(2)}, u32[]{:S(2)}) %collective-permute-start.31) | collective-permute-done | bytes 307232 | tf_op jit(solution)/shard_map/ppermute | solution.py:704
  362.1 3.9 collective-permute-done.32
  366.2 8.1 %collective-permute-done.33 = bf16[160,960]{1,0:T(8,128)(2,1)S(1)} collective-permute-done((bf16[160,960]{1,0:T(8,128)(2,1)S(1)}, bf16[160,960]{1,0:T(8,128)(2,1)S(1)}, u32[]{:S(2)}, u32[]{:S(2)}) %collective-permute-start.33) | collective-permute-done | bytes 307232 | tf_op jit(solution)/shard_map/ppermute | solution.py:653
  375.3 10.6 %shard_map.177 = bf16[4,336,1536]{2,1,0:T(8,128)(2,1)} custom-call(s32[1]{0:T(128)} %bitcast.here_ref, s32[1]{0:T(128)} %bitcast.1.place_ref, bf16[1280,960]{1,0:T(8,128)(2,1)} %get-tuple-element.115.whole_ref, bf16[1280,768]{1,0:T(8,128)(2,1)} %all-gather.3.cloned.1.call-done.normed_ref.refs_0_, ...), custom_call_target="tpu_custom_call" | custom-call | flops 3774873600 | bytes 16777216 | tf_op jit(solution)/shard_map/pallas_call | solution.py:603
  386.0 9.5 %shard_map.178 = (bf16[2,320,960]{2,1,0:T(8,128)(2,1)}, bf16[2,320,960]{2,1,0:T(8,128)(2,1)}, f32[1280,1]{1,0:T(8,128)}) custom-call(s32[1]{0:T(128)} %bitcast.1.place_ref, bf16[1280,960]{1,0:T(8,128)(2,1)} %get-tuple-element.115.whole_ref, bf16[1280,768]{1,0:T(8,128)(2,1)} %all-gather.3.cloned.1.call-done.normed_ref.refs_0_, ...), custom_call_target="tpu_custom_call" | custom-call | flops 3774873600 | bytes 12582912 | tf_op jit(solution)/shard_map/pallas_call | solution.py:634
  395.5 2.0 collective-permute-start.44
  397.8 1.6 collective-permute-start.36
  399.4 1.3 copy.71
  403.5 2.1 collective-permute-done.40
  406.6 2.0 collective-permute-done.41
  408.6 1.5 broadcast_in_dim.27
  410.9 20.7 %collective-permute-done.42 = f32[2640]{0:T(1024)S(1)} collective-permute-done((f32[2640]{0:T(1024)S(1)}, f32[2640]{0:T(1024)S(1)}, u32[]{:S(2)}, u32[]{:S(2)}) %collective-permute-start.42) | collective-permute-done | bytes 10592 | tf_op jit(solution)/shard_map/ppermute | solution.py:653
  431.7 2.2 fusion.6
  434.5 1.8 fusion.12
  438.3 9.9 %collective-permute-done.43 = f32[2640]{0:T(1024)S(1)} collective-permute-done((f32[2640]{0:T(1024)S(1)}, f32[2640]{0:T(1024)S(1)}, u32[]{:S(2)}, u32[]{:S(2)}) %collective-permute-start.43) | collective-permute-done | bytes 10592 | tf_op jit(solution)/shard_map/ppermute | solution.py:653
  449.7 1.8 fusion.4
  454.6 11.6 %collective-permute-done.46 = bf16[320,960]{1,0:T(8,128)(2,1)S(1)} collective-permute-done((bf16[320,960]{1,0:T(8,128)(2,1)S(1)}, bf16[320,960]{1,0:T(8,128)(2,1)S(1)}, u32[]{:S(2)}, u32[]{:S(2)}) %collective-permute-start.46) | collective-permute-done | bytes 614432 | tf_op jit(solution)/shard_map/ppermute | solution.py:653
  466.3 1.3 convert_add_fusion
  467.6 1.8 copy.74
  470.6 3.1 copy.77
  473.6 8.7 %reduce-scatter.2.cloned.1.call-done = bf16[1,336,1536]{2,1,0:T(8,128)(2,1)} async-done(((bf16[4,336,1536]{2,1,0:T(8,128)(2,1)}), bf16[1,336,1536]{2,1,0:T(8,128)(2,1)}) %reduce-scatter.2.cloned.1.call-update) | async-done | bytes 1032208 | tf_op jit(solution)/shard_map/reduce_scatter | solution.py:864
  482.3 1.6 convert_element_type.156
  484.1 1.7 fusion.3
  (166 shorter events, 42.6 us)
Async XLA Ops:
  7.2 7.9 %copy-start = (f32[1536,320]{0,1:T(8,128)S(1)}, f32[1536,320]{0,1:T(8,128)}, u32[]{:S(2)}) copy-start(f32[1536,320]{0,1:T(8,128)} %param.10) | copy-start | bytes 5898244
  7.2 7.9 %copy-start.13 = (f32[320]{0:T(512)S(1)}, f32[320]{0:T(512)}, u32[]{:S(2)}) copy-start(f32[320]{0:T(512)} %param.12) | copy-start | bytes 3844
  7.2 89.8 %all-gather.3.cloned.1.call-start = ((), (), s32[]{:S(2)}) async-start(), calls=%async_computation.3 | async-start | bytes 2457600 | tf_op jit(solution)/shard_map/all_gather | solution.py:779
  9.1 2.6 collective-permute-start.3
  11.7 3.4 collective-permute-start.4
  16.3 111.8 %all-gather.5.cloned.1.call-start = ((), (), s32[]{:S(2)}) async-start(), calls=%async_computation.4 | async-start | bytes 2457600 | tf_op jit(solution)/shard_map/all_gather | solution.py:779
  19.3 13.6 %collective-permute-start.1 = (bf16[320,960]{1,0:T(8,128)(2,1)}, bf16[320,960]{1,0:T(8,128)(2,1)}, u32[]{:S(2)}, u32[]{:S(2)}) collective-permute-start(bf16[320,960]{1,0:T(8,128)(2,1)} %copy.64.refs_0_), channel_id=1, source_target_pairs={{0,8},{4,12},{8,0},{12,4},{1,9},{5,13},{9,1},{13,5},{2,10},{6,14},... | collective-permute-start | bytes 1843208 | tf_op jit(solution)/shard_map/ppermute | solution.py:653
  20.5 18.9 %collective-permute-start = (bf16[320,960]{1,0:T(8,128)(2,1)}, bf16[320,960]{1,0:T(8,128)(2,1)}, u32[]{:S(2)}, u32[]{:S(2)}) collective-permute-start(bf16[320,960]{1,0:T(8,128)(2,1)} %copy.64.refs_0_), channel_id=1, source_target_pairs={{0,4},{4,0},{8,12},{12,8},{1,5},{5,1},{9,13},{13,9},{2,6},{6,2},{1... | collective-permute-start | bytes 1843208 | tf_op jit(solution)/shard_map/ppermute | solution.py:653
  32.9 6.6 %collective-permute-start.2 = (bf16[320,960]{1,0:T(8,128)(2,1)}, bf16[320,960]{1,0:T(8,128)(2,1)}, u32[]{:S(2)}, u32[]{:S(2)}) collective-permute-start(bf16[320,960]{1,0:T(8,128)(2,1)} %collective-permute-done.1.refs_2_), channel_id=1, source_target_pairs={{0,4},{4,0},{8,12},{12,8},{1,5},{5,1},{9,13},{13,9},{2,6},{6,2},{1... | collective-permute-start | bytes 1843208 | tf_op jit(solution)/shard_map/ppermute | solution.py:653
  39.5 4.5 copy-start.10
  45.6 50.3 %copy-start.17 = (f32[80]{0:T(128)S(1)}, f32[80]{0:T(128)}, u32[]{:S(2)}) copy-start(f32[80]{0:T(128)} %param.14) | copy-start | bytes 964
  45.8 37.6 %collective-permute-start.6 = (bf16[176,960]{1,0:T(8,128)(2,1)S(1)}, bf16[176,960]{1,0:T(8,128)(2,1)S(1)}, u32[]{:S(2)}, u32[]{:S(2)}) collective-permute-start(bf16[176,960]{1,0:T(8,128)(2,1)S(1)} %maximum_maximum_fusion), channel_id=1, source_target_pairs={{0,2},{1,3},{2,0},{3,1},{4,6},{5,7},{6,4},{7,5},{8,10},{9,11},{10,... | collective-permute-start | bytes 1013768 | tf_op jit(solution)/shard_map/ppermute | solution.py:704
  48.2 45.2 %collective-permute-start.7 = (bf16[176,960]{1,0:T(8,128)(2,1)S(1)}, bf16[176,960]{1,0:T(8,128)(2,1)S(1)}, u32[]{:S(2)}, u32[]{:S(2)}) collective-permute-start(bf16[176,960]{1,0:T(8,128)(2,1)S(1)} %maximum_maximum_fusion), channel_id=1, source_target_pairs={{0,3},{1,0},{2,1},{3,2},{4,7},{5,4},{6,5},{7,6},{8,11},{9,8},{10,9... | collective-permute-start | bytes 1013768 | tf_op jit(solution)/shard_map/ppermute | solution.py:704
  48.3 45.0 %collective-permute-start.5 = (bf16[176,960]{1,0:T(8,128)(2,1)S(1)}, bf16[176,960]{1,0:T(8,128)(2,1)S(1)}, u32[]{:S(2)}, u32[]{:S(2)}) collective-permute-start(bf16[176,960]{1,0:T(8,128)(2,1)S(1)} %maximum_maximum_fusion), channel_id=1, source_target_pairs={{0,1},{1,2},{2,3},{3,0},{4,5},{5,6},{6,7},{7,4},{8,9},{9,10},{10,1... | collective-permute-start | bytes 1013768 | tf_op jit(solution)/shard_map/ppermute | solution.py:704
  93.5 111.1 %copy-start.2 = (bf16[4,176,960]{2,1,0:T(8,128)(2,1)}, bf16[4,176,960]{2,1,0:T(8,128)(2,1)S(1)}, u32[]{:S(2)}) copy-start(bf16[4,176,960]{2,1,0:T(8,128)(2,1)S(1)} %pad_maximum_fusion.refs_0_) | copy-start | bytes 4055044
  93.5 40.2 %collective-permute-start.8 = (bf16[4,176,960]{2,1,0:T(8,128)(2,1)S(1)}, bf16[4,176,960]{2,1,0:T(8,128)(2,1)}, u32[]{:S(2)}, u32[]{:S(2)}) collective-permute-start(bf16[4,176,960]{2,1,0:T(8,128)(2,1)S(1)} %pad_maximum_fusion.refs_0_), channel_id=1, source_target_pairs={{0,16},{16,0},{1,17},{17,1},{2,18},{18,2},{3,19},{19,3},{4,20},{20... | collective-permute-start | bytes 4055048 | tf_op jit(solution)/shard_map/ppermute | solution.py:653
  94.8 39.9 %collective-permute-start.9 = (bf16[4,176,960]{2,1,0:T(8,128)(2,1)S(1)}, bf16[4,176,960]{2,1,0:T(8,128)(2,1)}, u32[]{:S(2)}, u32[]{:S(2)}) collective-permute-start(bf16[4,176,960]{2,1,0:T(8,128)(2,1)S(1)} %pad_maximum_fusion.refs_0_), channel_id=1, source_target_pairs={{0,8},{4,12},{8,0},{12,4},{1,9},{5,13},{9,1},{13,5},{2,10},{6,14},... | collective-permute-start | bytes 4055048 | tf_op jit(solution)/shard_map/ppermute | solution.py:653
  102.7 33.2 %collective-permute-start.10 = (bf16[240,768]{1,0:T(8,128)(2,1)}, bf16[240,768]{1,0:T(8,128)(2,1)}, u32[]{:S(2)}, u32[]{:S(2)}) collective-permute-start(bf16[240,768]{1,0:T(8,128)(2,1)} %get-tuple-element.69), channel_id=1, source_target_pairs={{0,4},{4,0},{8,12},{12,8},{1,5},{5,1},{9,13},{13,9},{2,6},{6,2},{1... | collective-permute-start | bytes 1105928 | tf_op jit(solution)/shard_map/ppermute | solution.py:653
  103.7 34.3 %collective-permute-start.11 = (bf16[240,768]{1,0:T(8,128)(2,1)}, bf16[240,768]{1,0:T(8,128)(2,1)}, u32[]{:S(2)}, u32[]{:S(2)}) collective-permute-start(bf16[240,768]{1,0:T(8,128)(2,1)} %get-tuple-element.70), channel_id=1, source_target_pairs={{0,8},{4,12},{8,0},{12,4},{1,9},{5,13},{9,1},{13,5},{2,10},{6,14},... | collective-permute-start | bytes 1105928 | tf_op jit(solution)/shard_map/ppermute | solution.py:653
  104.0 41.5 %collective-permute-start.12 = (bf16[240,768]{1,0:T(8,128)(2,1)}, bf16[240,768]{1,0:T(8,128)(2,1)}, u32[]{:S(2)}, u32[]{:S(2)}) collective-permute-start(bf16[240,768]{1,0:T(8,128)(2,1)} %get-tuple-element.71), channel_id=1, source_target_pairs={{0,12},{4,8},{8,4},{12,0},{1,13},{5,9},{9,5},{13,1},{2,14},{6,10},... | collective-permute-start | bytes 1105928 | tf_op jit(solution)/shard_map/ppermute | solution.py:653
  133.8 11.7 %collective-permute-start.13 = (bf16[240,768]{1,0:T(8,128)(2,1)}, bf16[240,768]{1,0:T(8,128)(2,1)}, u32[]{:S(2)}, u32[]{:S(2)}) collective-permute-start(bf16[240,768]{1,0:T(8,128)(2,1)} %get-tuple-element.74), channel_id=1, source_target_pairs={{0,4},{4,0},{8,12},{12,8},{1,5},{5,1},{9,13},{13,9},{2,6},{6,2},{1... | collective-permute-start | bytes 1105928 | tf_op jit(solution)/shard_map/ppermute | solution.py:653
  134.7 16.3 %collective-permute-start.14 = (bf16[240,768]{1,0:T(8,128)(2,1)}, bf16[240,768]{1,0:T(8,128)(2,1)}, u32[]{:S(2)}, u32[]{:S(2)}) collective-permute-start(bf16[240,768]{1,0:T(8,128)(2,1)} %get-tuple-element.75), channel_id=1, source_target_pairs={{0,8},{4,12},{8,0},{12,4},{1,9},{5,13},{9,1},{13,5},{2,10},{6,14},... | collective-permute-start | bytes 1105928 | tf_op jit(solution)/shard_map/ppermute | solution.py:653
  135.9 24.2 %collective-permute-start.15 = (bf16[240,768]{1,0:T(8,128)(2,1)}, bf16[240,768]{1,0:T(8,128)(2,1)}, u32[]{:S(2)}, u32[]{:S(2)}) collective-permute-start(bf16[240,768]{1,0:T(8,128)(2,1)} %get-tuple-element.76), channel_id=1, source_target_pairs={{0,12},{4,8},{8,4},{12,0},{1,13},{5,9},{9,5},{13,1},{2,14},{6,10},... | collective-permute-start | bytes 1105928 | tf_op jit(solution)/shard_map/ppermute | solution.py:653
  138.0 60.5 %collective-permute-start.16 = (bf16[320,384]{1,0:T(8,128)(2,1)}, bf16[320,384]{1,0:T(8,128)(2,1)}, u32[]{:S(2)}, u32[]{:S(2)}) collective-permute-start(bf16[320,384]{1,0:T(8,128)(2,1)} %get-tuple-element.167), channel_id=1, source_target_pairs={{0,1},{1,2},{2,3},{3,0},{4,5},{5,6},{6,7},{7,4},{8,9},{9,10},{10,1... | collective-permute-start | bytes 737288 | tf_op jit(solution)/shard_map/ppermute | solution.py:704
  145.5 53.0 %collective-permute-start.17 = (bf16[320,384]{1,0:T(8,128)(2,1)}, bf16[320,384]{1,0:T(8,128)(2,1)}, u32[]{:S(2)}, u32[]{:S(2)}) collective-permute-start(bf16[320,384]{1,0:T(8,128)(2,1)} %get-tuple-element.166), channel_id=1, source_target_pairs={{0,2},{1,3},{2,0},{3,1},{4,6},{5,7},{6,4},{7,5},{8,10},{9,11},{10,... | collective-permute-start | bytes 737288 | tf_op jit(solution)/shard_map/ppermute | solution.py:704
  145.5 53.0 %collective-permute-start.18 = (bf16[320,384]{1,0:T(8,128)(2,1)}, bf16[320,384]{1,0:T(8,128)(2,1)}, u32[]{:S(2)}, u32[]{:S(2)}) collective-permute-start(bf16[320,384]{1,0:T(8,128)(2,1)} %get-tuple-element.165), channel_id=1, source_target_pairs={{0,3},{1,0},{2,1},{3,2},{4,7},{5,4},{6,5},{7,6},{8,11},{9,8},{10,9... | collective-permute-start | bytes 737288 | tf_op jit(solution)/shard_map/ppermute | solution.py:704
  151.0 51.9 %collective-permute-start.21 = (bf16[4,176,960]{2,1,0:T(8,128)(2,1)}, bf16[4,176,960]{2,1,0:T(8,128)(2,1)}, u32[]{:S(2)}, u32[]{:S(2)}) collective-permute-start(bf16[4,176,960]{2,1,0:T(8,128)(2,1)} %collective-permute-done.9.refs_4_), channel_id=1, source_target_pairs={{0,16},{16,0},{1,17},{17,1},{2,18},{18,2},{3,19},{19,3},{4,20},{20... | collective-permute-start | bytes 4055048 | tf_op jit(solution)/shard_map/ppermute | solution.py:653
  198.5 26.3 %all-to-all-start = ((bf16[16,80,384]{2,1,0:T(8,128)(2,1)}), bf16[16,80,384]{2,1,0:T(8,128)(2,1)}, u32[]{:S(2)}, u32[]{:S(2)}) async-start(bf16[16,80,384]{2,1,0:T(8,128)(2,1)} %get-tuple-element.78), calls=%async_computation | async-start | bytes 1966080 | tf_op jit(solution)/shard_map/all_to_all | solution.py:802
  202.9 5.8 %collective-permute-start.23 = (bf16[4,176,960]{2,1,0:T(8,128)(2,1)}, bf16[4,176,960]{2,1,0:T(8,128)(2,1)}, u32[]{:S(2)}, u32[]{:S(2)}) collective-permute-start(bf16[4,176,960]{2,1,0:T(8,128)(2,1)} %collective-permute-done.21.refs_5_), channel_id=1, source_target_pairs={{0,4},{4,0},{8,12},{12,8},{1,5},{5,1},{9,13},{13,9},{2,6},{6,2},{1... | collective-permute-start | bytes 4055048 | tf_op jit(solution)/shard_map/ppermute | solution.py:653
  203.1 7.6 %collective-permute-start.22 = (bf16[4,176,960]{2,1,0:T(8,128)(2,1)}, bf16[4,176,960]{2,1,0:T(8,128)(2,1)}, u32[]{:S(2)}, u32[]{:S(2)}) collective-permute-start(bf16[4,176,960]{2,1,0:T(8,128)(2,1)} %collective-permute-done.9.refs_4_), channel_id=1, source_target_pairs={{0,4},{4,0},{8,12},{12,8},{1,5},{5,1},{9,13},{13,9},{2,6},{6,2},{1... | collective-permute-start | bytes 4055048 | tf_op jit(solution)/shard_map/ppermute | solution.py:653
  203.5 9.2 %collective-permute-start.20 = (bf16[4,176,960]{2,1,0:T(8,128)(2,1)}, bf16[4,176,960]{2,1,0:T(8,128)(2,1)}, u32[]{:S(2)}, u32[]{:S(2)}) collective-permute-start(bf16[4,176,960]{2,1,0:T(8,128)(2,1)} %collective-permute-done.8.refs_1_), channel_id=1, source_target_pairs={{0,4},{4,0},{8,12},{12,8},{1,5},{5,1},{9,13},{13,9},{2,6},{6,2},{1... | collective-permute-start | bytes 4055048 | tf_op jit(solution)/shard_map/ppermute | solution.py:653
  203.6 9.2 %collective-permute-start.19 = (bf16[4,176,960]{2,1,0:T(8,128)(2,1)S(1)}, bf16[4,176,960]{2,1,0:T(8,128)(2,1)}, u32[]{:S(2)}, u32[]{:S(2)}) collective-permute-start(bf16[4,176,960]{2,1,0:T(8,128)(2,1)S(1)} %pad_maximum_fusion.refs_0_), channel_id=1, source_target_pairs={{0,4},{4,0},{8,12},{12,8},{1,5},{5,1},{9,13},{13,9},{2,6},{6,2},{1... | collective-permute-start | bytes 4055048 | tf_op jit(solution)/shard_map/ppermute | solution.py:653
  242.4 10.7 %collective-permute-start.25 = (bf16[3,384,1280]{2,1,0:T(8,128)(2,1)}, bf16[3,384,1280]{2,1,0:T(8,128)(2,1)}, u32[]{:S(2)}, u32[]{:S(2)}) collective-permute-start(bf16[3,384,1280]{2,1,0:T(8,128)(2,1)} %get-tuple-element.91.refs_1_), channel_id=1, source_target_pairs={{0,4},{4,0},{8,12},{12,8},{1,5},{5,1},{9,13},{13,9},{2,6},{6,2},{1... | collective-permute-start | bytes 8847368 | tf_op jit(solution)/shard_map/ppermute | solution.py:653
  243.6 28.1 %all-to-all-start.1 = ((bf16[16,80,384]{2,1,0:T(8,128)(2,1)}), bf16[16,80,384]{2,1,0:T(8,128)(2,1)S(1)}, u32[]{:S(2)}, u32[]{:S(2)}) async-start(bf16[16,80,384]{2,1,0:T(8,128)(2,1)} %get-tuple-element.89), calls=%async_computation.1 | async-start | bytes 1966080 | tf_op jit(solution)/shard_map/all_to_all | solution.py:832
  249.4 232.9 %reduce-scatter.2.cloned.1.call-start = ((), (), s32[]{:S(2)}) async-start(), calls=%async_computation.5 | async-start | bytes 5160960 | tf_op jit(solution)/shard_map/reduce_scatter | solution.py:864
  249.4 3.7 collective-permute-start.24
  263.3 66.5 %collective-permute-start.27 = (bf16[4,160,960]{2,1,0:T(8,128)(2,1)}, bf16[4,160,960]{2,1,0:T(8,128)(2,1)}, u32[]{:S(2)}, u32[]{:S(2)}) collective-permute-start(bf16[4,160,960]{2,1,0:T(8,128)(2,1)} %get-tuple-element.94), channel_id=1, source_target_pairs={{0,16},{4,20},{8,24},{12,28},{16,0},{20,4},{24,8},{28,12},{1,17},{... | collective-permute-start | bytes 3686408 | tf_op jit(solution)/shard_map/ppermute | solution.py:661
  263.3 66.5 %collective-permute-start.28 = (bf16[4,160,960]{2,1,0:T(8,128)(2,1)}, bf16[4,160,960]{2,1,0:T(8,128)(2,1)}, u32[]{:S(2)}, u32[]{:S(2)}) collective-permute-start(bf16[4,160,960]{2,1,0:T(8,128)(2,1)} %get-tuple-element.95), channel_id=1, source_target_pairs={{0,8},{4,12},{8,0},{12,4},{16,24},{20,28},{24,16},{28,20},{1,9},{5... | collective-permute-start | bytes 3686408 | tf_op jit(solution)/shard_map/ppermute | solution.py:661
  264.6 65.2 %collective-permute-start.29 = (bf16[4,160,960]{2,1,0:T(8,128)(2,1)}, bf16[4,160,960]{2,1,0:T(8,128)(2,1)}, u32[]{:S(2)}, u32[]{:S(2)}) collective-permute-start(bf16[4,160,960]{2,1,0:T(8,128)(2,1)} %get-tuple-element.96), channel_id=1, source_target_pairs={{0,24},{4,28},{8,16},{12,20},{16,8},{20,12},{24,0},{28,4},{1,25},{... | collective-permute-start | bytes 3686408 | tf_op jit(solution)/shard_map/ppermute | solution.py:661
  272.6 57.2 %copy-start.4 = (bf16[4,160,960]{2,1,0:T(8,128)(2,1)S(1)}, bf16[4,160,960]{2,1,0:T(8,128)(2,1)}, u32[]{:S(2)}) copy-start(bf16[4,160,960]{2,1,0:T(8,128)(2,1)} %get-tuple-element.101) | copy-start | bytes 3686404
  326.7 3.1 collective-permute-start.26
  333.4 5.1 %copy-start.16 = (bf16[240,1536]{1,0:T(8,128)(2,1)S(1)}, bf16[240,1536]{1,0:T(8,128)(2,1)}, u32[]{:S(2)}) copy-start(bf16[240,1536]{1,0:T(8,128)(2,1)} %get-tuple-element.106) | copy-start | bytes 2211844
  333.4 5.6 %copy-start.15 = (bf16[240,1536]{1,0:T(8,128)(2,1)S(1)}, bf16[240,1536]{1,0:T(8,128)(2,1)}, u32[]{:S(2)}) copy-start(bf16[240,1536]{1,0:T(8,128)(2,1)} %get-tuple-element.107) | copy-start | bytes 2211844
  333.5 10.3 %collective-permute-start.30 = (bf16[160,960]{1,0:T(8,128)(2,1)S(1)}, bf16[160,960]{1,0:T(8,128)(2,1)S(1)}, u32[]{:S(2)}, u32[]{:S(2)}) collective-permute-start(bf16[160,960]{1,0:T(8,128)(2,1)S(1)} %get-tuple-element.162), channel_id=1, source_target_pairs={{0,1},{1,2},{2,3},{3,0},{4,5},{5,6},{6,7},{7,4},{8,9},{9,10},{10,1... | collective-permute-start | bytes 921608 | tf_op jit(solution)/shard_map/ppermute | solution.py:704
  334.0 28.0 %collective-permute-start.31 = (bf16[160,960]{1,0:T(8,128)(2,1)S(1)}, bf16[160,960]{1,0:T(8,128)(2,1)S(1)}, u32[]{:S(2)}, u32[]{:S(2)}) collective-permute-start(bf16[160,960]{1,0:T(8,128)(2,1)S(1)} %get-tuple-element.164), channel_id=1, source_target_pairs={{0,2},{1,3},{2,0},{3,1},{4,6},{5,7},{6,4},{7,5},{8,10},{9,11},{10,... | collective-permute-start | bytes 921608 | tf_op jit(solution)/shard_map/ppermute | solution.py:704
  338.1 27.9 %collective-permute-start.32 = (bf16[160,960]{1,0:T(8,128)(2,1)S(1)}, bf16[160,960]{1,0:T(8,128)(2,1)S(1)}, u32[]{:S(2)}, u32[]{:S(2)}) collective-permute-start(bf16[160,960]{1,0:T(8,128)(2,1)S(1)} %get-tuple-element.163), channel_id=1, source_target_pairs={{0,3},{1,0},{2,1},{3,2},{4,7},{5,4},{6,5},{7,6},{8,11},{9,8},{10,9... | collective-permute-start | bytes 921608 | tf_op jit(solution)/shard_map/ppermute | solution.py:704
  338.5 35.9 %collective-permute-start.34 = (bf16[240,1536]{1,0:T(8,128)(2,1)S(1)}, bf16[240,1536]{1,0:T(8,128)(2,1)S(1)}, u32[]{:S(2)}, u32[]{:S(2)}) collective-permute-start(bf16[240,1536]{1,0:T(8,128)(2,1)S(1)} %copy-done.16), channel_id=1, source_target_pairs={{0,8},{4,12},{8,0},{12,4},{1,9},{5,13},{9,1},{13,5},{2,10},{6,14},... | collective-permute-start | bytes 2211848 | tf_op jit(solution)/shard_map/ppermute | solution.py:653
  339.0 35.4 %collective-permute-start.35 = (bf16[240,1536]{1,0:T(8,128)(2,1)S(1)}, bf16[240,1536]{1,0:T(8,128)(2,1)}, u32[]{:S(2)}, u32[]{:S(2)}) collective-permute-start(bf16[240,1536]{1,0:T(8,128)(2,1)S(1)} %copy-done.15), channel_id=1, source_target_pairs={{0,12},{4,8},{8,4},{12,0},{1,13},{5,9},{9,5},{13,1},{2,14},{6,10},... | collective-permute-start | bytes 2211848 | tf_op jit(solution)/shard_map/ppermute | solution.py:653
  366.2 8.2 %collective-permute-start.33 = (bf16[160,960]{1,0:T(8,128)(2,1)S(1)}, bf16[160,960]{1,0:T(8,128)(2,1)S(1)}, u32[]{:S(2)}, u32[]{:S(2)}) collective-permute-start(bf16[160,960]{1,0:T(8,128)(2,1)S(1)} %fusion.9), channel_id=1, source_target_pairs={{0,16},{16,0},{1,17},{17,1},{2,18},{18,2},{3,19},{19,3},{4,20},{20... | collective-permute-start | bytes 921608 | tf_op jit(solution)/shard_map/ppermute | solution.py:653
  386.0 11.5 %copy-start.8 = (f32[1280,1]{1,0:T(8,128)S(1)}, f32[1280,1]{1,0:T(8,128)}, u32[]{:S(2)}) copy-start(f32[1280,1]{1,0:T(8,128)} %get-tuple-element.117) | copy-start | bytes 15364
  386.0 11.7 %copy-start.12 = (f32[80,1]{1,0:T(8,128)S(1)}, f32[80,1]{1,0:T(8,128)}, u32[]{:S(2)}) copy-start(f32[80,1]{1,0:T(8,128)} %get-tuple-element.118) | copy-start | bytes 964
  395.5 36.2 %collective-permute-start.44 = (bf16[2,320,960]{2,1,0:T(8,128)(2,1)}, bf16[2,320,960]{2,1,0:T(8,128)(2,1)}, u32[]{:S(2)}, u32[]{:S(2)}) collective-permute-start(bf16[2,320,960]{2,1,0:T(8,128)(2,1)} %get-tuple-element.120), channel_id=1, source_target_pairs={{0,4},{4,0},{8,12},{12,8},{1,5},{5,1},{9,13},{13,9},{2,6},{6,2},{1... | collective-permute-start | bytes 3686408 | tf_op jit(solution)/shard_map/ppermute | solution.py:653
  397.8 56.0 %collective-permute-start.38 = (bf16[320,384]{1,0:T(8,128)(2,1)}, bf16[320,384]{1,0:T(8,128)(2,1)S(1)}, u32[]{:S(2)}, u32[]{:S(2)}) collective-permute-start(bf16[320,384]{1,0:T(8,128)(2,1)} %get-tuple-element.114), channel_id=1, source_target_pairs={{0,3},{1,0},{2,1},{3,2},{4,7},{5,4},{6,5},{7,6},{8,11},{9,8},{10,9... | collective-permute-start | bytes 737288 | tf_op jit(solution)/shard_map/ppermute | solution.py:704
  397.8 36.8 %collective-permute-start.36 = (bf16[320,384]{1,0:T(8,128)(2,1)}, bf16[320,384]{1,0:T(8,128)(2,1)}, u32[]{:S(2)}, u32[]{:S(2)}) collective-permute-start(bf16[320,384]{1,0:T(8,128)(2,1)} %get-tuple-element.110), channel_id=1, source_target_pairs={{0,1},{1,2},{2,3},{3,0},{4,5},{5,6},{6,7},{7,4},{8,9},{9,10},{10,1... | collective-permute-start | bytes 737288 | tf_op jit(solution)/shard_map/ppermute | solution.py:704
  400.8 1.8 collective-permute-start.39
  401.4 51.5 %collective-permute-start.37 = (bf16[320,384]{1,0:T(8,128)(2,1)}, bf16[320,384]{1,0:T(8,128)(2,1)S(1)}, u32[]{:S(2)}, u32[]{:S(2)}) collective-permute-start(bf16[320,384]{1,0:T(8,128)(2,1)} %get-tuple-element.112), channel_id=1, source_target_pairs={{0,2},{1,3},{2,0},{3,1},{4,6},{5,7},{6,4},{7,5},{8,10},{9,11},{10,... | collective-permute-start | bytes 737288 | tf_op jit(solution)/shard_map/ppermute | solution.py:704
  402.6 3.0 collective-permute-start.40
  405.6 4.5 copy-start.11
  405.6 2.9 collective-permute-start.41
  406.6 25.1 %copy-start.3 = (bf16[2,320,960]{2,1,0:T(8,128)(2,1)S(1)}, bf16[2,320,960]{2,1,0:T(8,128)(2,1)}, u32[]{:S(2)}) copy-start(bf16[2,320,960]{2,1,0:T(8,128)(2,1)} %get-tuple-element.119) | copy-start | bytes 3686404
  408.6 23.1 %collective-permute-start.42 = (f32[2640]{0:T(1024)S(1)}, f32[2640]{0:T(1024)S(1)}, u32[]{:S(2)}, u32[]{:S(2)}) collective-permute-start(f32[2640]{0:T(1024)S(1)} %add.197), channel_id=1, source_target_pairs={{0,1},{1,0},{2,3},{3,2},{4,5},{5,4},{6,7},{7,6},{8,9},{9,8},{10,11... | collective-permute-start | bytes 31688 | tf_op jit(solution)/shard_map/ppermute | solution.py:653
  431.7 16.6 %collective-permute-start.43 = (f32[2640]{0:T(1024)S(1)}, f32[2640]{0:T(1024)S(1)}, u32[]{:S(2)}, u32[]{:S(2)}) collective-permute-start(f32[2640]{0:T(1024)S(1)} %add.198), channel_id=1, source_target_pairs={{0,2},{1,3},{2,0},{3,1},{4,6},{5,7},{6,4},{7,5},{8,10},{9,11},{10,... | collective-permute-start | bytes 31688 | tf_op jit(solution)/shard_map/ppermute | solution.py:653
  433.9 15.8 %collective-permute-start.45 = (bf16[320,960]{1,0:T(8,128)(2,1)}, bf16[320,960]{1,0:T(8,128)(2,1)}, u32[]{:S(2)}, u32[]{:S(2)}) collective-permute-start(bf16[320,960]{1,0:T(8,128)(2,1)} %fusion.6), channel_id=1, source_target_pairs={{0,8},{4,12},{8,0},{12,4},{1,9},{5,13},{9,1},{13,5},{2,10},{6,14},... | collective-permute-start | bytes 1843208 | tf_op jit(solution)/shard_map/ppermute | solution.py:653
  451.5 14.8 %collective-permute-start.46 = (bf16[320,960]{1,0:T(8,128)(2,1)S(1)}, bf16[320,960]{1,0:T(8,128)(2,1)S(1)}, u32[]{:S(2)}, u32[]{:S(2)}) collective-permute-start(bf16[320,960]{1,0:T(8,128)(2,1)S(1)} %fusion.4), channel_id=1, source_target_pairs={{0,16},{16,0},{1,17},{17,1},{2,18},{18,2},{3,19},{19,3},{4,20},{20... | collective-permute-start | bytes 1843208 | tf_op jit(solution)/shard_map/ppermute | solution.py:653
  (6 other events, 13.1 us)
Sparse Core Ops, SparseCore 0:
  16.4 65.6 all-gather.2
  84.3 43.7 all-gather.4
  386.1 96.1 reduce-scatter.1
where the time goes:
time: 501 us; the launch traced here: 493 us
  waiting for transfers between devices  203 us (41%)
  Pallas kernels  166 us (33%)
  starting transfers between devices  56.4 us (11%)
  other arithmetic  27.2 us (5%)
  local copies, waits for them, and re-layouts  24.9 us (5%)
  between operations  14.5 us (3%)
    ppermute x32, waiting for transfers between devices, partner(): return lax.ppermute(values, axis, [(at, at ^ flip) for at in range(size)])  95.9 us
    ppermute x12, waiting for transfers between devices, ring_swap(): lax.ppermute(pieces[shift], 'col', [(at, (at + shift) % cols) for at in r...  68.5 us
    pallas_call x1, Pallas kernels, attend_back(): pl.pallas_call(functools.partial(backward_kernel, tokens=tokens, part=par...  54.1 us
    pallas_call x1, Pallas kernels, attend(): pl.pallas_call(functools.partial(forward_kernel, tokens=tokens, part=part...  38.4 us
    ppermute x32, starting transfers between devices, partner(): return lax.ppermute(values, axis, [(at, at ^ flip) for at in range(size)])  29.4 us
    all_gather x2, waiting for transfers between devices, on_device(): normed_parts.append(lax.all_gather(part, 'col', axis=0, tiled=True))  22.8 us
    pallas_call x1, Pallas kernels, feed_forward(): pl.pallas_call(functools.partial(feed_kernel, rows=rows, cols=cols, heads...  17.6 us
    ppermute x12, starting transfers between devices, ring_swap(): lax.ppermute(pieces[shift], 'col', [(at, (at + shift) % cols) for at in r...  14 us
  transfers between devices with their start and end apart: 52, of which 26 were waited for; matrix products, arithmetic and copies ran while one was open for 8% of the time, Pallas kernels for 28%

commit v1 on v0

--- a/solution.py
+++ b/solution.py
@@ -857,7 +857,8 @@
     else:
         shard = sum_groups(mine, groups)
 
-    arrived[0] = after(arrived[0], mine)
+    change = ring_swap([after(piece, go) for piece in change], cols)
+    arrived[0] = after(arrived[0], mine, *change)
     payload = project_back(
         here_of, place_of, whole, normed_parts, back_two, arrived, rows, cols, heads
     )
@@ -888,9 +889,6 @@
     gain_two_grad = lax.dynamic_slice_in_dim(small[D : 2 * D], here * width, width)
     scale_grad = small[2 * D :] / scale * (scale_base / math.sqrt(HD)) * jax.nn.sigmoid(per_dim)
 
-    change = ring_swap(
-        [after(piece, go if at % 2 else payload) for at, piece in enumerate(change)], cols
-    )
     output = jnp.zeros_like(residual_in)
     for shift, piece in enumerate(change):
         at = lax.rem(here + cols - shift, cols) * sub

time: 501 us -> 486 us (0.970)
  the two profiles are of different devices: /device:TPU:9 before, /device:TPU:0 now
where the time goes in v1:
time: 486 us; the launch traced here: 478 us
  waiting for transfers between devices  183 us (38%)
  Pallas kernels  148 us (30%)
  starting transfers between devices  79.9 us (16%)
  other arithmetic  27.7 us (6%)
  local copies, waits for them, and re-layouts  25.3 us (5%)
  between operations  14.5 us (3%)
    ppermute x12, waiting for transfers between devices, ring_swap(): lax.ppermute(pieces[shift], 'col', [(at, (at + shift) % cols) for at in r...  68.3 us
    ppermute x32, waiting for transfers between devices, partner(): return lax.ppermute(values, axis, [(at, at ^ flip) for at in range(size)])  54.6 us
    pallas_call x1, Pallas kernels, attend_back(): pl.pallas_call(functools.partial(backward_kernel, tokens=tokens, part=par...  41.4 us
    ppermute x12, starting transfers between devices, ring_swap(): lax.ppermute(pieces[shift], 'col', [(at, (at + shift) % cols) for at in r...  37.5 us
    pallas_call x1, Pallas kernels, attend(): pl.pallas_call(functools.partial(forward_kernel, tokens=tokens, part=part...  31.8 us
    all_gather x2, waiting for transfers between devices, on_device(): normed_parts.append(lax.all_gather(part, 'col', axis=0, tiled=True))  30.6 us
    ppermute x32, starting transfers between devices, partner(): return lax.ppermute(values, axis, [(at, at ^ flip) for at in range(size)])  25 us
    pallas_call x1, Pallas kernels, feed_forward(): pl.pallas_call(functools.partial(feed_kernel, rows=rows, cols=cols, heads...  17.8 us
  transfers between devices with their start and end apart: 52, of which 23 were waited for; matrix products, arithmetic and copies ran while one was open for 9% of the time, Pallas kernels for 25%

profile of v1, /device:TPU:0, one launch (start us, length us, event | category | flops | bytes accessed | tf_op | source)
XLA Modules:
  0.0 477.8 jit_solution(14272779801880756336)
XLA Ops:
  7.2 1.8 multiply_reduce_fusion
  9.1 3.1 collective-permute-start.3
  12.2 1.6 collective-permute-done.3
  13.8 3.0 collective-permute-start.4
  16.8 1.6 collective-permute-done.4
  19.8 1.7 copy.60
  22.7 1.9 collective-permute-start.1
  24.6 12.9 %collective-permute-done.1.refs_2_ = bf16[320,960]{1,0:T(8,128)(2,1)} collective-permute-done((bf16[320,960]{1,0:T(8,128)(2,1)}, bf16[320,960]{1,0:T(8,128)(2,1)}, u32[]{:S(2)}, u32[]{:S(2)}) %collective-permute-start.1) | collective-permute-done | bytes 614432 | tf_op jit(solution)/shard_map/ppermute | solution.py:653
  37.5 1.7 convert_element_type.144
  40.2 4.2 shard_map.169
  46.5 2.8 collective-permute-start.6
  51.3 28.8 %collective-permute-done.6 = bf16[176,960]{1,0:T(8,128)(2,1)S(1)} collective-permute-done((bf16[176,960]{1,0:T(8,128)(2,1)S(1)}, bf16[176,960]{1,0:T(8,128)(2,1)S(1)}, u32[]{:S(2)}, u32[]{:S(2)}) %collective-permute-start.6) | collective-permute-done | bytes 337952 | tf_op jit(solution)/shard_map/ppermute | solution.py:704
  80.1 8.5 %collective-permute-done.5 = bf16[176,960]{1,0:T(8,128)(2,1)S(1)} collective-permute-done((bf16[176,960]{1,0:T(8,128)(2,1)S(1)}, bf16[176,960]{1,0:T(8,128)(2,1)S(1)}, u32[]{:S(2)}, u32[]{:S(2)}) %collective-permute-start.5) | collective-permute-done | bytes 337952 | tf_op jit(solution)/shard_map/ppermute | solution.py:704
  88.8 1.5 collective-permute-start.8
  90.4 1.5 collective-permute-start.9
  92.9 5.9 %shard_map.170 = (bf16[240,768]{1,0:T(8,128)(2,1)}, bf16[240,768]{1,0:T(8,128)(2,1)}, bf16[240,768]{1,0:T(8,128)(2,1)}, bf16[240,768]{1,0:T(8,128)(2,1)}) custom-call(s32[1]{0:T(128)} %bitcast.1.place_ref, bf16[960,1280]{1,0:T(8,128)(2,1)} %get-tuple-element.65.turned_ref, f32[960,1]{1,0:T(8,128)} %broadcast_in_dim_tile.4.factor_ref, ...), custom_call_target="tpu_custom_call" | custom-call | flops 1887436800 | bytes 10485760 | tf_op jit(solution)/shard_map/pallas_call | solution.py:555
  99.1 1.6 collective-permute-start.12
  100.7 30.6 %all-gather.5.cloned.1.call-done.normed_ref.refs_1_ = bf16[1280,768]{1,0:T(8,128)(2,1)} async-done(((bf16[320,768]{1,0:T(8,128)(2,1)}), bf16[1280,768]{1,0:T(8,128)(2,1)}) %all-gather.5.cloned.1.call-update) | async-done | bytes 1966096 | tf_op jit(solution)/shard_map/all_gather | solution.py:779
  131.2 5.7 %shard_map.171 = (bf16[240,768]{1,0:T(8,128)(2,1)}, bf16[240,768]{1,0:T(8,128)(2,1)}, bf16[240,768]{1,0:T(8,128)(2,1)}, bf16[240,768]{1,0:T(8,128)(2,1)}) custom-call(s32[1]{0:T(128)} %bitcast.1.place_ref, bf16[960,1280]{1,0:T(8,128)(2,1)} %get-tuple-element.65.turned_ref, f32[960,1]{1,0:T(8,128)} %broadcast_in_dim_tile.4.factor_ref, ...), custom_call_target="tpu_custom_call" | custom-call | flops 1887436800 | bytes 10485760 | tf_op jit(solution)/shard_map/pallas_call | solution.py:555
  136.9 1.5 collective-permute-start.14
  140.5 6.5 %collective-permute-start.17 = (bf16[320,384]{1,0:T(8,128)(2,1)}, bf16[320,384]{1,0:T(8,128)(2,1)}, u32[]{:S(2)}, u32[]{:S(2)}) collective-permute-start(bf16[320,384]{1,0:T(8,128)(2,1)} %get-tuple-element.166), channel_id=1, source_target_pairs={{0,2},{1,3},{2,0},{3,1},{4,6},{5,7},{6,4},{7,5},{8,10},{9,11},{10,... | collective-permute-start | bytes 737288 | tf_op jit(solution)/shard_map/ppermute | solution.py:704
  146.9 2.7 collective-permute-start.18
  150.2 5.5 %collective-permute-done.15.refs_7_ = bf16[240,768]{1,0:T(8,128)(2,1)} collective-permute-done((bf16[240,768]{1,0:T(8,128)(2,1)}, bf16[240,768]{1,0:T(8,128)(2,1)}, u32[]{:S(2)}, u32[]{:S(2)}) %collective-permute-start.15) | collective-permute-done | bytes 368672 | tf_op jit(solution)/shard_map/ppermute | solution.py:653
  155.7 31.8 %shard_map.172 = (f32[4,80,1536]{2,1,0:T(8,128)}, f32[4,1,1536]{2,1,0:T(1,128)}, bf16[4,240,1536]{2,1,0:T(8,128)(2,1)}, bf16[16,80,384]{2,1,0:T(8,128)(2,1)}) custom-call(s32[24]{0:T(128)} %convert_reduce_fusion.starts_ref, s32[1]{0:T(128)} %bitcast.1.place_ref, bf16[240,768]{1,0:T(8,128)(2,1)} %get-tuple-element.68.refs_0_, ...), custom_call_target="tpu_custom_call" | custom-call | flops 14495514624 | bytes 12582912 | tf_op jit(solution)/shard_map/pallas_call | solution.py:229
  187.5 9.4 %all-to-all-start = ((bf16[16,80,384]{2,1,0:T(8,128)(2,1)}), bf16[16,80,384]{2,1,0:T(8,128)(2,1)}, u32[]{:S(2)}, u32[]{:S(2)}) async-start(bf16[16,80,384]{2,1,0:T(8,128)(2,1)} %get-tuple-element.78), calls=%async_computation | async-start | bytes 1966080 | tf_op jit(solution)/shard_map/all_to_all | solution.py:802
  200.1 2.7 dynamic-slice_select_fusion.normed_ref
  202.8 1.9 collective-permute-done.22.refs_6_
  204.7 2.1 collective-permute-done.20.refs_3_
  206.8 10.5 %shard_map.173.w_hbm = bf16[3,1280,1280]{2,1,0:T(8,128)(2,1)} custom-call(s32[1]{0:T(128)} %bitcast.here_ref, s32[1]{0:T(128)} %bitcast.1.place_ref, s32[1]{0:T(128)} %bitcast.21.group_ref, bf16[4,176,960]{2,1,0:T(8,128)(2,1)} %copy-done.2, bf16[4,176,960]{2,1,0:T(8,128)(2,1)} %collective-permute-done.8.refs_1_, ...), custom_call_target="tpu_custom_call" | custom-call | bytes 20971520 | tf_op jit(solution)/shard_map/pallas_call | solution.py:458
  217.2 5.1 %all-to-all-done.att_ref = bf16[16,80,384]{2,1,0:T(8,128)(2,1)} async-done(((bf16[16,80,384]{2,1,0:T(8,128)(2,1)}), bf16[16,80,384]{2,1,0:T(8,128)(2,1)}, u32[]{:S(2)}, u32[]{:S(2)}) %all-to-all-start) | async-done | bytes 983072 | tf_op jit(solution)/shard_map/all_to_all | solution.py:802
  222.4 17.8 %shard_map.174 = (bf16[320,384]{1,0:T(8,128)(2,1)}, bf16[320,384]{1,0:T(8,128)(2,1)}, bf16[320,384]{1,0:T(8,128)(2,1)}, bf16[320,384]{1,0:T(8,128)(2,1)}, bf16[1...) custom-call(s32[1]{0:T(128)} %bitcast.here_ref, ...), custom_call_target="tpu_custom_call" | custom-call | flops 7549747200 | bytes 20971520 | tf_op jit(solution)/shard_map/pallas_call | solution.py:472
  240.3 3.7 all-to-all-start.1
  245.2 3.0 collective-permute-done.24.refs_2_
  248.2 10.2 %shard_map.175 = (bf16[4,160,960]{2,1,0:T(8,128)(2,1)}, bf16[4,160,960]{2,1,0:T(8,128)(2,1)}, bf16[4,160,960]{2,1,0:T(8,128)(2,1)}, bf16[4,160,960]{2,1,0:T(8,128)(2,1)}) custom-call(s32[1]{0:T(128)} %bitcast.here_ref, s32[1]{0:T(128)} %bitcast.21.group_ref, bf16[2,3,320,384]{3,2,1,0:T(8,128)(2,1)} %get-tuple-element.87.refs_0_, ...), custom_call_target="tpu_custom_call" | custom-call | flops 3774873600 | bytes 16777216 | tf_op jit(solution)/shard_map/pallas_call | solution.py:505
  258.4 2.8 collective-permute-start.30
  262.6 6.9 %all-to-all-done.1.go_ref = bf16[16,80,384]{2,1,0:T(8,128)(2,1)S(1)} async-done(((bf16[16,80,384]{2,1,0:T(8,128)(2,1)}), bf16[16,80,384]{2,1,0:T(8,128)(2,1)S(1)}, u32[]{:S(2)}, u32[]{:S(2)}) %all-to-all-start.1) | async-done | bytes 983072 | tf_op jit(solution)/shard_map/all_to_all | solution.py:832
  270.4 41.4 %shard_map.176 = (bf16[240,1536]{1,0:T(8,128)(2,1)}, bf16[240,1536]{1,0:T(8,128)(2,1)}, bf16[240,1536]{1,0:T(8,128)(2,1)}, bf16[240,1536]{1,0:T(8,128)(2,1)}, f32[80,1]{1,0:T(8,128)}) custom-call(s32[24]{0:T(128)} %convert_reduce_fusion.starts_ref, s32[1]{0:T(128)} %bitcast.1.place_ref, f32[80,1]{1,0:T(8,128)} %copy.70.scale_ref, ...), custom_call_target="tpu_custom_call" | custom-call | flops 38654705664 | bytes 16777216 | tf_op jit(solution)/shard_map/pallas_call | solution.py:253
  311.8 2.4 collective-permute-done.29.refs_4_.refs_3_
  314.2 6.5 %collective-permute-done.31 = bf16[4,160,960]{2,1,0:T(8,128)(2,1)} collective-permute-done((bf16[4,160,960]{2,1,0:T(8,128)(2,1)}, bf16[4,160,960]{2,1,0:T(8,128)(2,1)}, u32[]{:S(2)}, u32[]{:S(2)}) %collective-permute-start.31) | collective-permute-done | bytes 1228832 | tf_op jit(solution)/shard_map/ppermute | solution.py:661
  320.7 3.3 add_convert_fusion
  324.2 2.1 collective-permute-start.33
  326.3 1.8 collective-permute-start.34
  328.1 2.8 collective-permute-start.35
  331.5 5.3 %collective-permute-done.33 = bf16[160,960]{1,0:T(8,128)(2,1)S(1)} collective-permute-done((bf16[160,960]{1,0:T(8,128)(2,1)S(1)}, bf16[160,960]{1,0:T(8,128)(2,1)S(1)}, u32[]{:S(2)}, u32[]{:S(2)}) %collective-permute-start.33) | collective-permute-done | bytes 307232 | tf_op jit(solution)/shard_map/ppermute | solution.py:704
  336.8 12.0 %collective-permute-done.34 = bf16[160,960]{1,0:T(8,128)(2,1)S(1)} collective-permute-done((bf16[160,960]{1,0:T(8,128)(2,1)S(1)}, bf16[160,960]{1,0:T(8,128)(2,1)S(1)}, u32[]{:S(2)}, u32[]{:S(2)}) %collective-permute-start.34) | collective-permute-done | bytes 307232 | tf_op jit(solution)/shard_map/ppermute | solution.py:704
  349.8 10.0 %collective-permute-start.28 = (bf16[320,384]{1,0:T(8,128)(2,1)S(1)}, bf16[320,384]{1,0:T(8,128)(2,1)S(1)}, u32[]{:S(2)}, u32[]{:S(2)}) collective-permute-start(bf16[320,384]{1,0:T(8,128)(2,1)S(1)} %copy-done.24), channel_id=1, source_target_pairs={{0,3},{1,0},{2,1},{3,2},{4,7},{5,4},{6,5},{7,6},{8,11},{9,8},{10,9... | collective-permute-start | bytes 737288 | tf_op jit(solution)/shard_map/ppermute | solution.py:704
  359.9 6.6 %collective-permute-start.26 = (bf16[320,384]{1,0:T(8,128)(2,1)S(1)}, bf16[320,384]{1,0:T(8,128)(2,1)S(1)}, u32[]{:S(2)}, u32[]{:S(2)}) collective-permute-start(bf16[320,384]{1,0:T(8,128)(2,1)S(1)} %copy-done.22), channel_id=1, source_target_pairs={{0,1},{1,2},{2,3},{3,0},{4,5},{5,6},{6,7},{7,4},{8,9},{9,10},{10,1... | collective-permute-start | bytes 737288 | tf_op jit(solution)/shard_map/ppermute | solution.py:704
  366.6 13.7 %collective-permute-done.27 = bf16[320,384]{1,0:T(8,128)(2,1)S(1)} collective-permute-done((bf16[320,384]{1,0:T(8,128)(2,1)S(1)}, bf16[320,384]{1,0:T(8,128)(2,1)S(1)}, u32[]{:S(2)}, u32[]{:S(2)}) %collective-permute-start.27) | collective-permute-done | bytes 245792 | tf_op jit(solution)/shard_map/ppermute | solution.py:704
  381.3 10.7 %shard_map.177 = bf16[4,336,1536]{2,1,0:T(8,128)(2,1)} custom-call(s32[1]{0:T(128)} %bitcast.here_ref, s32[1]{0:T(128)} %bitcast.1.place_ref, bf16[1280,960]{1,0:T(8,128)(2,1)} %get-tuple-element.115.whole_ref, bf16[1280,768]{1,0:T(8,128)(2,1)} %all-gather.3.cloned.1.call-done.normed_ref.refs_0_, ...), custom_call_target="tpu_custom_call" | custom-call | flops 3774873600 | bytes 16777216 | tf_op jit(solution)/shard_map/pallas_call | solution.py:603
  392.0 9.5 %shard_map.178 = (bf16[2,320,960]{2,1,0:T(8,128)(2,1)}, bf16[2,320,960]{2,1,0:T(8,128)(2,1)}, f32[1280,1]{1,0:T(8,128)}) custom-call(s32[1]{0:T(128)} %bitcast.1.place_ref, bf16[1280,960]{1,0:T(8,128)(2,1)} %get-tuple-element.115.whole_ref, bf16[1280,768]{1,0:T(8,128)(2,1)} %all-gather.3.cloned.1.call-done.normed_ref.refs_0_, ...), custom_call_target="tpu_custom_call" | custom-call | flops 3774873600 | bytes 12582912 | tf_op jit(solution)/shard_map/pallas_call | solution.py:634
  402.5 1.5 broadcast_in_dim.27
  408.0 1.8 fusion.11
  411.6 1.9 collective-permute-done.40
  414.8 2.2 fusion.6
  418.7 3.9 collective-permute-done.42
  422.7 1.7 collective-permute-start.43
  427.6 5.3 %collective-permute-done.45 = bf16[320,960]{1,0:T(8,128)(2,1)} collective-permute-done((bf16[320,960]{1,0:T(8,128)(2,1)}, bf16[320,960]{1,0:T(8,128)(2,1)}, u32[]{:S(2)}, u32[]{:S(2)}) %collective-permute-start.45) | collective-permute-done | bytes 614432 | tf_op jit(solution)/shard_map/ppermute | solution.py:653
  432.9 1.8 fusion.4
  437.4 12.1 %collective-permute-done.46 = bf16[320,960]{1,0:T(8,128)(2,1)S(1)} collective-permute-done((bf16[320,960]{1,0:T(8,128)(2,1)S(1)}, bf16[320,960]{1,0:T(8,128)(2,1)S(1)}, u32[]{:S(2)}, u32[]{:S(2)}) %collective-permute-start.46) | collective-permute-done | bytes 614432 | tf_op jit(solution)/shard_map/ppermute | solution.py:653
  450.8 1.8 copy.74
  453.8 3.0 copy.77
  456.8 10.7 %reduce-scatter.2.cloned.1.call-done = bf16[1,336,1536]{2,1,0:T(8,128)(2,1)} async-done(((bf16[4,336,1536]{2,1,0:T(8,128)(2,1)}), bf16[1,336,1536]{2,1,0:T(8,128)(2,1)}) %reduce-scatter.2.cloned.1.call-update) | async-done | bytes 1032208 | tf_op jit(solution)/shard_map/reduce_scatter | solution.py:865
  467.5 1.6 convert_element_type.156
  469.4 1.7 fusion.3
  (184 shorter events, 39.9 us)
Async XLA Ops:
  7.2 11.3 %copy-start = (f32[1536,320]{0,1:T(8,128)S(1)}, f32[1536,320]{0,1:T(8,128)}, u32[]{:S(2)}) copy-start(f32[1536,320]{0,1:T(8,128)} %param.10) | copy-start | bytes 5898244
  7.2 11.3 %copy-start.18 = (f32[320]{0:T(512)S(1)}, f32[320]{0:T(512)}, u32[]{:S(2)}) copy-start(f32[320]{0:T(512)} %param.12) | copy-start | bytes 3844
  7.2 85.7 %all-gather.3.cloned.1.call-start = ((), (), s32[]{:S(2)}) async-start(), calls=%async_computation.3 | async-start | bytes 2457600 | tf_op jit(solution)/shard_map/all_gather | solution.py:779
  9.1 4.7 collective-permute-start.3
  13.8 4.7 collective-permute-start.4
  19.7 111.5 %all-gather.5.cloned.1.call-start = ((), (), s32[]{:S(2)}) async-start(), calls=%async_computation.4 | async-start | bytes 2457600 | tf_op jit(solution)/shard_map/all_gather | solution.py:779
  22.7 14.8 %collective-permute-start.1 = (bf16[320,960]{1,0:T(8,128)(2,1)}, bf16[320,960]{1,0:T(8,128)(2,1)}, u32[]{:S(2)}, u32[]{:S(2)}) collective-permute-start(bf16[320,960]{1,0:T(8,128)(2,1)} %copy.64.refs_0_), channel_id=1, source_target_pairs={{0,8},{4,12},{8,0},{12,4},{1,9},{5,13},{9,1},{13,5},{2,10},{6,14},... | collective-permute-start | bytes 1843208 | tf_op jit(solution)/shard_map/ppermute | solution.py:653
  24.6 15.6 %collective-permute-start = (bf16[320,960]{1,0:T(8,128)(2,1)}, bf16[320,960]{1,0:T(8,128)(2,1)}, u32[]{:S(2)}, u32[]{:S(2)}) collective-permute-start(bf16[320,960]{1,0:T(8,128)(2,1)} %copy.64.refs_0_), channel_id=1, source_target_pairs={{0,4},{4,0},{8,12},{12,8},{1,5},{5,1},{9,13},{13,9},{2,6},{6,2},{1... | collective-permute-start | bytes 1843208 | tf_op jit(solution)/shard_map/ppermute | solution.py:653
  37.5 2.7 collective-permute-start.2
  46.4 45.5 %copy-start.25 = (f32[80]{0:T(128)S(1)}, f32[80]{0:T(128)}, u32[]{:S(2)}) copy-start(f32[80]{0:T(128)} %param.14) | copy-start | bytes 964
  46.5 33.6 %collective-permute-start.6 = (bf16[176,960]{1,0:T(8,128)(2,1)S(1)}, bf16[176,960]{1,0:T(8,128)(2,1)S(1)}, u32[]{:S(2)}, u32[]{:S(2)}) collective-permute-start(bf16[176,960]{1,0:T(8,128)(2,1)S(1)} %maximum_maximum_fusion), channel_id=1, source_target_pairs={{0,2},{1,3},{2,0},{3,1},{4,6},{5,7},{6,4},{7,5},{8,10},{9,11},{10,... | collective-permute-start | bytes 1013768 | tf_op jit(solution)/shard_map/ppermute | solution.py:704
  49.3 30.9 %collective-permute-start.7 = (bf16[176,960]{1,0:T(8,128)(2,1)S(1)}, bf16[176,960]{1,0:T(8,128)(2,1)S(1)}, u32[]{:S(2)}, u32[]{:S(2)}) collective-permute-start(bf16[176,960]{1,0:T(8,128)(2,1)S(1)} %maximum_maximum_fusion), channel_id=1, source_target_pairs={{0,3},{1,0},{2,1},{3,2},{4,7},{5,4},{6,5},{7,6},{8,11},{9,8},{10,9... | collective-permute-start | bytes 1013768 | tf_op jit(solution)/shard_map/ppermute | solution.py:704
  50.6 38.0 %collective-permute-start.5 = (bf16[176,960]{1,0:T(8,128)(2,1)S(1)}, bf16[176,960]{1,0:T(8,128)(2,1)S(1)}, u32[]{:S(2)}, u32[]{:S(2)}) collective-permute-start(bf16[176,960]{1,0:T(8,128)(2,1)S(1)} %maximum_maximum_fusion), channel_id=1, source_target_pairs={{0,1},{1,2},{2,3},{3,0},{4,5},{5,6},{6,7},{7,4},{8,9},{9,10},{10,1... | collective-permute-start | bytes 1013768 | tf_op jit(solution)/shard_map/ppermute | solution.py:704
  88.8 109.8 %copy-start.2 = (bf16[4,176,960]{2,1,0:T(8,128)(2,1)}, bf16[4,176,960]{2,1,0:T(8,128)(2,1)S(1)}, u32[]{:S(2)}) copy-start(bf16[4,176,960]{2,1,0:T(8,128)(2,1)S(1)} %pad_maximum_fusion.refs_0_) | copy-start | bytes 4055044
  88.8 48.1 %collective-permute-start.8 = (bf16[4,176,960]{2,1,0:T(8,128)(2,1)S(1)}, bf16[4,176,960]{2,1,0:T(8,128)(2,1)}, u32[]{:S(2)}, u32[]{:S(2)}) collective-permute-start(bf16[4,176,960]{2,1,0:T(8,128)(2,1)S(1)} %pad_maximum_fusion.refs_0_), channel_id=1, source_target_pairs={{0,16},{16,0},{1,17},{17,1},{2,18},{18,2},{3,19},{19,3},{4,20},{20... | collective-permute-start | bytes 4055048 | tf_op jit(solution)/shard_map/ppermute | solution.py:653
  90.4 46.5 %collective-permute-start.9 = (bf16[4,176,960]{2,1,0:T(8,128)(2,1)S(1)}, bf16[4,176,960]{2,1,0:T(8,128)(2,1)}, u32[]{:S(2)}, u32[]{:S(2)}) collective-permute-start(bf16[4,176,960]{2,1,0:T(8,128)(2,1)S(1)} %pad_maximum_fusion.refs_0_), channel_id=1, source_target_pairs={{0,8},{4,12},{8,0},{12,4},{1,9},{5,13},{9,1},{13,5},{2,10},{6,14},... | collective-permute-start | bytes 4055048 | tf_op jit(solution)/shard_map/ppermute | solution.py:653
  98.8 39.7 %collective-permute-start.10 = (bf16[240,768]{1,0:T(8,128)(2,1)}, bf16[240,768]{1,0:T(8,128)(2,1)}, u32[]{:S(2)}, u32[]{:S(2)}) collective-permute-start(bf16[240,768]{1,0:T(8,128)(2,1)} %get-tuple-element.69), channel_id=1, source_target_pairs={{0,4},{4,0},{8,12},{12,8},{1,5},{5,1},{9,13},{13,9},{2,6},{6,2},{1... | collective-permute-start | bytes 1105928 | tf_op jit(solution)/shard_map/ppermute | solution.py:653
  98.8 41.5 %collective-permute-start.11 = (bf16[240,768]{1,0:T(8,128)(2,1)}, bf16[240,768]{1,0:T(8,128)(2,1)}, u32[]{:S(2)}, u32[]{:S(2)}) collective-permute-start(bf16[240,768]{1,0:T(8,128)(2,1)} %get-tuple-element.70), channel_id=1, source_target_pairs={{0,8},{4,12},{8,0},{12,4},{1,9},{5,13},{9,1},{13,5},{2,10},{6,14},... | collective-permute-start | bytes 1105928 | tf_op jit(solution)/shard_map/ppermute | solution.py:653
  99.1 41.4 %collective-permute-start.12 = (bf16[240,768]{1,0:T(8,128)(2,1)}, bf16[240,768]{1,0:T(8,128)(2,1)}, u32[]{:S(2)}, u32[]{:S(2)}) collective-permute-start(bf16[240,768]{1,0:T(8,128)(2,1)} %get-tuple-element.71), channel_id=1, source_target_pairs={{0,12},{4,8},{8,4},{12,0},{1,13},{5,9},{9,5},{13,1},{2,14},{6,10},... | collective-permute-start | bytes 1105928 | tf_op jit(solution)/shard_map/ppermute | solution.py:653
  136.9 10.0 %collective-permute-start.13 = (bf16[240,768]{1,0:T(8,128)(2,1)}, bf16[240,768]{1,0:T(8,128)(2,1)}, u32[]{:S(2)}, u32[]{:S(2)}) collective-permute-start(bf16[240,768]{1,0:T(8,128)(2,1)} %get-tuple-element.74), channel_id=1, source_target_pairs={{0,4},{4,0},{8,12},{12,8},{1,5},{5,1},{9,13},{13,9},{2,6},{6,2},{1... | collective-permute-start | bytes 1105928 | tf_op jit(solution)/shard_map/ppermute | solution.py:653
  136.9 12.7 %collective-permute-start.14 = (bf16[240,768]{1,0:T(8,128)(2,1)}, bf16[240,768]{1,0:T(8,128)(2,1)}, u32[]{:S(2)}, u32[]{:S(2)}) collective-permute-start(bf16[240,768]{1,0:T(8,128)(2,1)} %get-tuple-element.75), channel_id=1, source_target_pairs={{0,8},{4,12},{8,0},{12,4},{1,9},{5,13},{9,1},{13,5},{2,10},{6,14},... | collective-permute-start | bytes 1105928 | tf_op jit(solution)/shard_map/ppermute | solution.py:653
  138.5 17.2 %collective-permute-start.15 = (bf16[240,768]{1,0:T(8,128)(2,1)}, bf16[240,768]{1,0:T(8,128)(2,1)}, u32[]{:S(2)}, u32[]{:S(2)}) collective-permute-start(bf16[240,768]{1,0:T(8,128)(2,1)} %get-tuple-element.76), channel_id=1, source_target_pairs={{0,12},{4,8},{8,4},{12,0},{1,13},{5,9},{9,5},{13,1},{2,14},{6,10},... | collective-permute-start | bytes 1105928 | tf_op jit(solution)/shard_map/ppermute | solution.py:653
  140.3 47.2 %collective-permute-start.16 = (bf16[320,384]{1,0:T(8,128)(2,1)}, bf16[320,384]{1,0:T(8,128)(2,1)}, u32[]{:S(2)}, u32[]{:S(2)}) collective-permute-start(bf16[320,384]{1,0:T(8,128)(2,1)} %get-tuple-element.167), channel_id=1, source_target_pairs={{0,1},{1,2},{2,3},{3,0},{4,5},{5,6},{6,7},{7,4},{8,9},{9,10},{10,1... | collective-permute-start | bytes 737288 | tf_op jit(solution)/shard_map/ppermute | solution.py:704
  140.5 47.0 %collective-permute-start.17 = (bf16[320,384]{1,0:T(8,128)(2,1)}, bf16[320,384]{1,0:T(8,128)(2,1)}, u32[]{:S(2)}, u32[]{:S(2)}) collective-permute-start(bf16[320,384]{1,0:T(8,128)(2,1)} %get-tuple-element.166), channel_id=1, source_target_pairs={{0,2},{1,3},{2,0},{3,1},{4,6},{5,7},{6,4},{7,5},{8,10},{9,11},{10,... | collective-permute-start | bytes 737288 | tf_op jit(solution)/shard_map/ppermute | solution.py:704
  146.9 40.6 %collective-permute-start.18 = (bf16[320,384]{1,0:T(8,128)(2,1)}, bf16[320,384]{1,0:T(8,128)(2,1)}, u32[]{:S(2)}, u32[]{:S(2)}) collective-permute-start(bf16[320,384]{1,0:T(8,128)(2,1)} %get-tuple-element.165), channel_id=1, source_target_pairs={{0,3},{1,0},{2,1},{3,2},{4,7},{5,4},{6,5},{7,6},{8,11},{9,8},{10,9... | collective-permute-start | bytes 737288 | tf_op jit(solution)/shard_map/ppermute | solution.py:704
  149.6 47.3 %collective-permute-start.21 = (bf16[4,176,960]{2,1,0:T(8,128)(2,1)}, bf16[4,176,960]{2,1,0:T(8,128)(2,1)}, u32[]{:S(2)}, u32[]{:S(2)}) collective-permute-start(bf16[4,176,960]{2,1,0:T(8,128)(2,1)} %collective-permute-done.9.refs_4_), channel_id=1, source_target_pairs={{0,16},{16,0},{1,17},{17,1},{2,18},{18,2},{3,19},{19,3},{4,20},{20... | collective-permute-start | bytes 4055048 | tf_op jit(solution)/shard_map/ppermute | solution.py:653
  187.5 34.9 %all-to-all-start = ((bf16[16,80,384]{2,1,0:T(8,128)(2,1)}), bf16[16,80,384]{2,1,0:T(8,128)(2,1)}, u32[]{:S(2)}, u32[]{:S(2)}) async-start(bf16[16,80,384]{2,1,0:T(8,128)(2,1)} %get-tuple-element.78), calls=%async_computation | async-start | bytes 1966080 | tf_op jit(solution)/shard_map/all_to_all | solution.py:802
  196.9 5.8 %collective-permute-start.23 = (bf16[4,176,960]{2,1,0:T(8,128)(2,1)}, bf16[4,176,960]{2,1,0:T(8,128)(2,1)}, u32[]{:S(2)}, u32[]{:S(2)}) collective-permute-start(bf16[4,176,960]{2,1,0:T(8,128)(2,1)} %collective-permute-done.21.refs_5_), channel_id=1, source_target_pairs={{0,4},{4,0},{8,12},{12,8},{1,5},{5,1},{9,13},{13,9},{2,6},{6,2},{1... | collective-permute-start | bytes 4055048 | tf_op jit(solution)/shard_map/ppermute | solution.py:653
  197.3 7.3 %collective-permute-start.22 = (bf16[4,176,960]{2,1,0:T(8,128)(2,1)}, bf16[4,176,960]{2,1,0:T(8,128)(2,1)}, u32[]{:S(2)}, u32[]{:S(2)}) collective-permute-start(bf16[4,176,960]{2,1,0:T(8,128)(2,1)} %collective-permute-done.9.refs_4_), channel_id=1, source_target_pairs={{0,4},{4,0},{8,12},{12,8},{1,5},{5,1},{9,13},{13,9},{2,6},{6,2},{1... | collective-permute-start | bytes 4055048 | tf_op jit(solution)/shard_map/ppermute | solution.py:653
  197.5 9.2 %collective-permute-start.20 = (bf16[4,176,960]{2,1,0:T(8,128)(2,1)}, bf16[4,176,960]{2,1,0:T(8,128)(2,1)}, u32[]{:S(2)}, u32[]{:S(2)}) collective-permute-start(bf16[4,176,960]{2,1,0:T(8,128)(2,1)} %collective-permute-done.8.refs_1_), channel_id=1, source_target_pairs={{0,4},{4,0},{8,12},{12,8},{1,5},{5,1},{9,13},{13,9},{2,6},{6,2},{1... | collective-permute-start | bytes 4055048 | tf_op jit(solution)/shard_map/ppermute | solution.py:653
  197.9 8.9 %collective-permute-start.19 = (bf16[4,176,960]{2,1,0:T(8,128)(2,1)S(1)}, bf16[4,176,960]{2,1,0:T(8,128)(2,1)}, u32[]{:S(2)}, u32[]{:S(2)}) collective-permute-start(bf16[4,176,960]{2,1,0:T(8,128)(2,1)S(1)} %pad_maximum_fusion.refs_0_), channel_id=1, source_target_pairs={{0,4},{4,0},{8,12},{12,8},{1,5},{5,1},{9,13},{13,9},{2,6},{6,2},{1... | collective-permute-start | bytes 4055048 | tf_op jit(solution)/shard_map/ppermute | solution.py:653
  240.2 8.0 %collective-permute-start.25 = (bf16[3,384,1280]{2,1,0:T(8,128)(2,1)}, bf16[3,384,1280]{2,1,0:T(8,128)(2,1)}, u32[]{:S(2)}, u32[]{:S(2)}) collective-permute-start(bf16[3,384,1280]{2,1,0:T(8,128)(2,1)} %get-tuple-element.88.refs_1_), channel_id=1, source_target_pairs={{0,4},{4,0},{8,12},{12,8},{1,5},{5,1},{9,13},{13,9},{2,6},{6,2},{1... | collective-permute-start | bytes 8847368 | tf_op jit(solution)/shard_map/ppermute | solution.py:653
  240.3 29.2 %all-to-all-start.1 = ((bf16[16,80,384]{2,1,0:T(8,128)(2,1)}), bf16[16,80,384]{2,1,0:T(8,128)(2,1)S(1)}, u32[]{:S(2)}, u32[]{:S(2)}) async-start(bf16[16,80,384]{2,1,0:T(8,128)(2,1)} %get-tuple-element.86), calls=%async_computation.1 | async-start | bytes 1966080 | tf_op jit(solution)/shard_map/all_to_all | solution.py:832
  243.9 223.6 %reduce-scatter.2.cloned.1.call-start = ((), (), s32[]{:S(2)}) async-start(), calls=%async_computation.5 | async-start | bytes 5160960 | tf_op jit(solution)/shard_map/reduce_scatter | solution.py:865
  244.0 4.2 collective-permute-start.24
  258.4 55.9 %collective-permute-start.30 = (bf16[4,160,960]{2,1,0:T(8,128)(2,1)}, bf16[4,160,960]{2,1,0:T(8,128)(2,1)}, u32[]{:S(2)}, u32[]{:S(2)}) collective-permute-start(bf16[4,160,960]{2,1,0:T(8,128)(2,1)} %get-tuple-element.91), channel_id=1, source_target_pairs={{0,16},{4,20},{8,24},{12,28},{16,0},{20,4},{24,8},{28,12},{1,17},{... | collective-permute-start | bytes 3686408 | tf_op jit(solution)/shard_map/ppermute | solution.py:661
  261.1 59.6 %collective-permute-start.31 = (bf16[4,160,960]{2,1,0:T(8,128)(2,1)}, bf16[4,160,960]{2,1,0:T(8,128)(2,1)}, u32[]{:S(2)}, u32[]{:S(2)}) collective-permute-start(bf16[4,160,960]{2,1,0:T(8,128)(2,1)} %get-tuple-element.92), channel_id=1, source_target_pairs={{0,8},{4,12},{8,0},{12,4},{16,24},{20,28},{24,16},{28,20},{1,9},{5... | collective-permute-start | bytes 3686408 | tf_op jit(solution)/shard_map/ppermute | solution.py:661
  262.5 58.3 %collective-permute-start.32 = (bf16[4,160,960]{2,1,0:T(8,128)(2,1)}, bf16[4,160,960]{2,1,0:T(8,128)(2,1)}, u32[]{:S(2)}, u32[]{:S(2)}) collective-permute-start(bf16[4,160,960]{2,1,0:T(8,128)(2,1)} %get-tuple-element.93), channel_id=1, source_target_pairs={{0,24},{4,28},{8,16},{12,20},{16,8},{20,12},{24,0},{28,4},{1,25},{... | collective-permute-start | bytes 3686408 | tf_op jit(solution)/shard_map/ppermute | solution.py:661
  270.4 50.3 %copy-start.4 = (bf16[4,160,960]{2,1,0:T(8,128)(2,1)S(1)}, bf16[4,160,960]{2,1,0:T(8,128)(2,1)}, u32[]{:S(2)}) copy-start(bf16[4,160,960]{2,1,0:T(8,128)(2,1)} %get-tuple-element.108) | copy-start | bytes 3686404
  311.8 2.4 collective-permute-start.29
  314.2 9.8 %copy-start.6 = (bf16[240,1536]{1,0:T(8,128)(2,1)}, bf16[240,1536]{1,0:T(8,128)(2,1)S(1)}, u32[]{:S(2)}) copy-start(bf16[240,1536]{1,0:T(8,128)(2,1)S(1)} %collective-permute-done.29.refs_4_.refs_3_) | copy-start | bytes 2211844
  324.1 25.8 %copy-start.24 = (bf16[320,384]{1,0:T(8,128)(2,1)S(1)}, bf16[320,384]{1,0:T(8,128)(2,1)}, u32[]{:S(2)}) copy-start(bf16[320,384]{1,0:T(8,128)(2,1)} %get-tuple-element.101) | copy-start | bytes 737284
  324.1 35.8 %copy-start.23 = (bf16[320,384]{1,0:T(8,128)(2,1)S(1)}, bf16[320,384]{1,0:T(8,128)(2,1)}, u32[]{:S(2)}) copy-start(bf16[320,384]{1,0:T(8,128)(2,1)} %get-tuple-element.99) | copy-start | bytes 737284
  324.1 35.8 %copy-start.22 = (bf16[320,384]{1,0:T(8,128)(2,1)S(1)}, bf16[320,384]{1,0:T(8,128)(2,1)}, u32[]{:S(2)}) copy-start(bf16[320,384]{1,0:T(8,128)(2,1)} %get-tuple-element.97) | copy-start | bytes 737284
  324.2 12.6 %collective-permute-start.33 = (bf16[160,960]{1,0:T(8,128)(2,1)S(1)}, bf16[160,960]{1,0:T(8,128)(2,1)S(1)}, u32[]{:S(2)}, u32[]{:S(2)}) collective-permute-start(bf16[160,960]{1,0:T(8,128)(2,1)S(1)} %get-tuple-element.162), channel_id=1, source_target_pairs={{0,1},{1,2},{2,3},{3,0},{4,5},{5,6},{6,7},{7,4},{8,9},{9,10},{10,1... | collective-permute-start | bytes 921608 | tf_op jit(solution)/shard_map/ppermute | solution.py:704
  326.3 22.5 %collective-permute-start.34 = (bf16[160,960]{1,0:T(8,128)(2,1)S(1)}, bf16[160,960]{1,0:T(8,128)(2,1)S(1)}, u32[]{:S(2)}, u32[]{:S(2)}) collective-permute-start(bf16[160,960]{1,0:T(8,128)(2,1)S(1)} %get-tuple-element.164), channel_id=1, source_target_pairs={{0,2},{1,3},{2,0},{3,1},{4,6},{5,7},{6,4},{7,5},{8,10},{9,11},{10,... | collective-permute-start | bytes 921608 | tf_op jit(solution)/shard_map/ppermute | solution.py:704
  328.1 20.8 %collective-permute-start.35 = (bf16[160,960]{1,0:T(8,128)(2,1)S(1)}, bf16[160,960]{1,0:T(8,128)(2,1)S(1)}, u32[]{:S(2)}, u32[]{:S(2)}) collective-permute-start(bf16[160,960]{1,0:T(8,128)(2,1)S(1)} %get-tuple-element.163), channel_id=1, source_target_pairs={{0,3},{1,0},{2,1},{3,2},{4,7},{5,4},{6,5},{7,6},{8,11},{9,8},{10,9... | collective-permute-start | bytes 921608 | tf_op jit(solution)/shard_map/ppermute | solution.py:704
  330.9 49.4 %collective-permute-start.37 = (bf16[240,1536]{1,0:T(8,128)(2,1)S(1)}, bf16[240,1536]{1,0:T(8,128)(2,1)S(1)}, u32[]{:S(2)}, u32[]{:S(2)}) collective-permute-start(bf16[240,1536]{1,0:T(8,128)(2,1)S(1)} %copy-done.21), channel_id=1, source_target_pairs={{0,8},{4,12},{8,0},{12,4},{1,9},{5,13},{9,1},{13,5},{2,10},{6,14},... | collective-permute-start | bytes 2211848 | tf_op jit(solution)/shard_map/ppermute | solution.py:653
  331.5 48.8 %collective-permute-start.38 = (bf16[240,1536]{1,0:T(8,128)(2,1)S(1)}, bf16[240,1536]{1,0:T(8,128)(2,1)}, u32[]{:S(2)}, u32[]{:S(2)}) collective-permute-start(bf16[240,1536]{1,0:T(8,128)(2,1)S(1)} %copy-done.20), channel_id=1, source_target_pairs={{0,12},{4,8},{8,4},{12,0},{1,13},{5,9},{9,5},{13,1},{2,14},{6,10},... | collective-permute-start | bytes 2211848 | tf_op jit(solution)/shard_map/ppermute | solution.py:653
  349.0 10.8 %collective-permute-start.36 = (bf16[160,960]{1,0:T(8,128)(2,1)S(1)}, bf16[160,960]{1,0:T(8,128)(2,1)S(1)}, u32[]{:S(2)}, u32[]{:S(2)}) collective-permute-start(bf16[160,960]{1,0:T(8,128)(2,1)S(1)} %fusion.9), channel_id=1, source_target_pairs={{0,16},{16,0},{1,17},{17,1},{2,18},{18,2},{3,19},{19,3},{4,20},{20... | collective-permute-start | bytes 921608 | tf_op jit(solution)/shard_map/ppermute | solution.py:653
  349.8 16.7 %collective-permute-start.28 = (bf16[320,384]{1,0:T(8,128)(2,1)S(1)}, bf16[320,384]{1,0:T(8,128)(2,1)S(1)}, u32[]{:S(2)}, u32[]{:S(2)}) collective-permute-start(bf16[320,384]{1,0:T(8,128)(2,1)S(1)} %copy-done.24), channel_id=1, source_target_pairs={{0,3},{1,0},{2,1},{3,2},{4,7},{5,4},{6,5},{7,6},{8,11},{9,8},{10,9... | collective-permute-start | bytes 737288 | tf_op jit(solution)/shard_map/ppermute | solution.py:704
  359.9 20.4 %collective-permute-start.27 = (bf16[320,384]{1,0:T(8,128)(2,1)S(1)}, bf16[320,384]{1,0:T(8,128)(2,1)S(1)}, u32[]{:S(2)}, u32[]{:S(2)}) collective-permute-start(bf16[320,384]{1,0:T(8,128)(2,1)S(1)} %copy-done.23), channel_id=1, source_target_pairs={{0,2},{1,3},{2,0},{3,1},{4,6},{5,7},{6,4},{7,5},{8,10},{9,11},{10,... | collective-permute-start | bytes 737288 | tf_op jit(solution)/shard_map/ppermute | solution.py:704
  359.9 20.4 %collective-permute-start.26 = (bf16[320,384]{1,0:T(8,128)(2,1)S(1)}, bf16[320,384]{1,0:T(8,128)(2,1)S(1)}, u32[]{:S(2)}, u32[]{:S(2)}) collective-permute-start(bf16[320,384]{1,0:T(8,128)(2,1)S(1)} %copy-done.22), channel_id=1, source_target_pairs={{0,1},{1,2},{2,3},{3,0},{4,5},{5,6},{6,7},{7,4},{8,9},{9,10},{10,1... | collective-permute-start | bytes 737288 | tf_op jit(solution)/shard_map/ppermute | solution.py:704
  366.6 13.7 %copy-start.13 = (bf16[320,384]{1,0:T(8,128)(2,1)}, bf16[320,384]{1,0:T(8,128)(2,1)S(1)}, u32[]{:S(2)}) copy-start(bf16[320,384]{1,0:T(8,128)(2,1)S(1)} %collective-permute-done.28) | copy-start | bytes 737284
  392.0 9.5 %copy-start.8 = (f32[1280,1]{1,0:T(8,128)S(1)}, f32[1280,1]{1,0:T(8,128)}, u32[]{:S(2)}) copy-start(f32[1280,1]{1,0:T(8,128)} %get-tuple-element.117) | copy-start | bytes 15364
  401.5 13.3 %collective-permute-start.44 = (bf16[2,320,960]{2,1,0:T(8,128)(2,1)}, bf16[2,320,960]{2,1,0:T(8,128)(2,1)}, u32[]{:S(2)}, u32[]{:S(2)}) collective-permute-start(bf16[2,320,960]{2,1,0:T(8,128)(2,1)} %get-tuple-element.120), channel_id=1, source_target_pairs={{0,4},{4,0},{8,12},{12,8},{1,5},{5,1},{9,13},{13,9},{2,6},{6,2},{1... | collective-permute-start | bytes 3686408 | tf_op jit(solution)/shard_map/ppermute | solution.py:653
  407.4 2.4 collective-permute-start.39
  409.8 3.7 collective-permute-start.40
  413.5 5.0 %collective-permute-start.41 = (f32[2640]{0:T(1024)S(1)}, f32[2640]{0:T(1024)S(1)}, u32[]{:S(2)}, u32[]{:S(2)}) collective-permute-start(f32[2640]{0:T(1024)S(1)} %add.196), channel_id=1, source_target_pairs={{0,16},{16,0},{1,17},{17,1},{2,18},{18,2},{3,19},{19,3},{4,20},{20... | collective-permute-start | bytes 31688 | tf_op jit(solution)/shard_map/ppermute | solution.py:653
  416.9 15.9 %collective-permute-start.45 = (bf16[320,960]{1,0:T(8,128)(2,1)}, bf16[320,960]{1,0:T(8,128)(2,1)}, u32[]{:S(2)}, u32[]{:S(2)}) collective-permute-start(bf16[320,960]{1,0:T(8,128)(2,1)} %fusion.6), channel_id=1, source_target_pairs={{0,8},{4,12},{8,0},{12,4},{1,9},{5,13},{9,1},{13,5},{2,10},{6,14},... | collective-permute-start | bytes 1843208 | tf_op jit(solution)/shard_map/ppermute | solution.py:653
  418.5 4.2 collective-permute-start.42
  422.7 4.9 %collective-permute-start.43 = (f32[2640]{0:T(1024)S(1)}, f32[2640]{0:T(1024)S(1)}, u32[]{:S(2)}, u32[]{:S(2)}) collective-permute-start(f32[2640]{0:T(1024)S(1)} %add.198), channel_id=1, source_target_pairs={{0,2},{1,3},{2,0},{3,1},{4,6},{5,7},{6,4},{7,5},{8,10},{9,11},{10,... | collective-permute-start | bytes 31688 | tf_op jit(solution)/shard_map/ppermute | solution.py:653
  426.3 10.5 %copy-start.26 = (f32[80]{0:T(128)S(1)}, f32[80]{0:T(128)}, u32[]{:S(2)}) copy-start(f32[80]{0:T(128)} %param.14) | copy-start | bytes 964
  434.7 14.8 %collective-permute-start.46 = (bf16[320,960]{1,0:T(8,128)(2,1)S(1)}, bf16[320,960]{1,0:T(8,128)(2,1)S(1)}, u32[]{:S(2)}, u32[]{:S(2)}) collective-permute-start(bf16[320,960]{1,0:T(8,128)(2,1)S(1)} %fusion.4), channel_id=1, source_target_pairs={{0,16},{16,0},{1,17},{17,1},{2,18},{18,2},{3,19},{19,3},{4,20},{20... | collective-permute-start | bytes 1843208 | tf_op jit(solution)/shard_map/ppermute | solution.py:653
  (15 other events, 52.2 us)
Sparse Core Ops, SparseCore 0:
  19.9 60.1 all-gather.2
  82.2 48.9 all-gather.4
  392.1 75.3 reduce-scatter.1

commit v2 on v1

--- a/solution.py
+++ b/solution.py
@@ -110,29 +110,26 @@
         query = padded([qkv_ref[source, 0:HD, pl.ds(at, tile)], bias], tile)
 
         def key_tile(key_number, state):
-            largest, total, result = state
+            largest, result = state
             keys = key_scr[pl.ds(pl.multiple_of(key_number * tile, tile), tile), :]
             scores = dot(keys, query)
             key_at = pl.multiple_of((key_number % per_part) * tile, tile)
             values = qkv_ref[key_number // per_part, 2 * HD : 3 * HD, pl.ds(key_at, tile)]
+            values = jnp.concatenate([values, jnp.ones((16, tile), bf16)], axis=0)
             newest = jnp.maximum(largest, jnp.max(scores, axis=0, keepdims=True))
             factor = jnp.exp(largest - newest)
             weights = jnp.exp(scores - newest)
-            total = total * factor + jnp.sum(weights, axis=0, keepdims=True)
             result = result * factor + dot(values, weights.astype(bf16))
-            return newest, total, result
-
-        largest, total, result = lax.fori_loop(
+            return newest, result
+
+        largest, result = lax.fori_loop(
             starts_ref[number * per_tile] // per_tile,
             number + 1,
             key_tile,
-            (
-                jnp.full((1, tile), -jnp.inf, f32),
-                jnp.zeros((1, tile), f32),
-                jnp.zeros((HD, tile), f32),
-            ),
+            (jnp.full((1, tile), -jnp.inf, f32), jnp.zeros((HD + 16, tile), f32)),
         )
-        result = result / total
+        total = result[HD : HD + 1]
+        result = result[:HD] / total
         out_ref[source, :, pl.ds(at, tile)] = result
         store_pieces(leave_ref, result.astype(bf16), source, number % per_part, part)
         lse_ref[source, :, pl.ds(at, tile)] = largest + jnp.log(total)

time: 486 us -> 490 us (level)
  starting transfers between devices: 79.9 us -> 85.3 us
    ppermute x32, starting transfers between devices: 25 us -> 30.9 us  [partner(): return lax.ppermute(values, axis, [(at, at ^ flip) for at in range(size)])]
  transfers between devices with their start and end apart: 52 -> 52, of which waited for: 23 -> 24; matrix products, arithmetic and copies ran while one was open for 9% -> 8% of each run, Pallas kernels for 25% -> 25%
where the time goes in v2:
time: 490 us; the launch traced here: 487 us
  waiting for transfers between devices  183 us (37%)
  Pallas kernels  151 us (31%)
  starting transfers between devices  85.3 us (17%)
  other arithmetic  27.7 us (6%)
  local copies, waits for them, and re-layouts  25.3 us (5%)
  between operations  14.5 us (3%)
    ppermute x12, waiting for transfers between devices, ring_swap(): lax.ppermute(pieces[shift], 'col', [(at, (at + shift) % cols) for at in r...  71.2 us
    ppermute x32, waiting for transfers between devices, partner(): return lax.ppermute(values, axis, [(at, at ^ flip) for at in range(size)])  57.9 us
    pallas_call x1, Pallas kernels, attend_back(): pl.pallas_call(functools.partial(backward_kernel, tokens=tokens, part=par...  45.1 us
    ppermute x12, starting transfers between devices, ring_swap(): lax.ppermute(pieces[shift], 'col', [(at, (at + shift) % cols) for at in r...  32.9 us
    pallas_call x1, Pallas kernels, attend(): pl.pallas_call(functools.partial(forward_kernel, tokens=tokens, part=part...  31 us
    ppermute x32, starting transfers between devices, partner(): return lax.ppermute(values, axis, [(at, at ^ flip) for at in range(size)])  30.9 us
    all_gather x2, waiting for transfers between devices, on_device(): normed_parts.append(lax.all_gather(part, 'col', axis=0, tiled=True))  30.6 us
    pallas_call x1, Pallas kernels, feed_forward(): pl.pallas_call(functools.partial(feed_kernel, rows=rows, cols=cols, heads...  17.8 us
  transfers between devices with their start and end apart: 52, of which 24 were waited for; matrix products, arithmetic and copies ran while one was open for 8% of the time, Pallas kernels for 25%

profile of v2, /device:TPU:0, one launch (start us, length us, event | category | flops | bytes accessed | tf_op | source)
XLA Modules:
  0.0 486.6 jit_solution(13882123663575481767)
XLA Ops:
  7.2 1.8 multiply_reduce_fusion
  9.1 3.1 collective-permute-start.3
  12.2 1.6 collective-permute-done.3
  13.8 3.0 collective-permute-start.4
  16.8 1.6 collective-permute-done.4
  19.8 1.7 copy.60
  22.7 1.9 collective-permute-start.1
  24.6 12.9 %collective-permute-done.1.refs_2_ = bf16[320,960]{1,0:T(8,128)(2,1)} collective-permute-done((bf16[320,960]{1,0:T(8,128)(2,1)}, bf16[320,960]{1,0:T(8,128)(2,1)}, u32[]{:S(2)}, u32[]{:S(2)}) %collective-permute-start.1) | collective-permute-done | bytes 614432 | tf_op jit(solution)/shard_map/ppermute | solution.py:650
  37.5 1.7 convert_element_type.144
  40.2 4.2 shard_map.169
  46.5 2.8 collective-permute-start.6
  51.3 28.8 %collective-permute-done.6 = bf16[176,960]{1,0:T(8,128)(2,1)S(1)} collective-permute-done((bf16[176,960]{1,0:T(8,128)(2,1)S(1)}, bf16[176,960]{1,0:T(8,128)(2,1)S(1)}, u32[]{:S(2)}, u32[]{:S(2)}) %collective-permute-start.6) | collective-permute-done | bytes 337952 | tf_op jit(solution)/shard_map/ppermute | solution.py:701
  80.1 8.5 %collective-permute-done.5 = bf16[176,960]{1,0:T(8,128)(2,1)S(1)} collective-permute-done((bf16[176,960]{1,0:T(8,128)(2,1)S(1)}, bf16[176,960]{1,0:T(8,128)(2,1)S(1)}, u32[]{:S(2)}, u32[]{:S(2)}) %collective-permute-start.5) | collective-permute-done | bytes 337952 | tf_op jit(solution)/shard_map/ppermute | solution.py:701
  88.8 1.5 collective-permute-start.8
  92.9 5.9 %shard_map.170 = (bf16[240,768]{1,0:T(8,128)(2,1)}, bf16[240,768]{1,0:T(8,128)(2,1)}, bf16[240,768]{1,0:T(8,128)(2,1)}, bf16[240,768]{1,0:T(8,128)(2,1)}) custom-call(s32[1]{0:T(128)} %bitcast.1.place_ref, bf16[960,1280]{1,0:T(8,128)(2,1)} %get-tuple-element.65.turned_ref, f32[960,1]{1,0:T(8,128)} %broadcast_in_dim_tile.4.factor_ref, ...), custom_call_target="tpu_custom_call" | custom-call | flops 1887436800 | bytes 10485760 | tf_op jit(solution)/shard_map/pallas_call | solution.py:552
  99.1 1.6 collective-permute-start.12
  100.7 30.6 %all-gather.5.cloned.1.call-done.normed_ref.refs_1_ = bf16[1280,768]{1,0:T(8,128)(2,1)} async-done(((bf16[320,768]{1,0:T(8,128)(2,1)}), bf16[1280,768]{1,0:T(8,128)(2,1)}) %all-gather.5.cloned.1.call-update) | async-done | bytes 1966096 | tf_op jit(solution)/shard_map/all_gather | solution.py:776
  131.2 5.7 %shard_map.171 = (bf16[240,768]{1,0:T(8,128)(2,1)}, bf16[240,768]{1,0:T(8,128)(2,1)}, bf16[240,768]{1,0:T(8,128)(2,1)}, bf16[240,768]{1,0:T(8,128)(2,1)}) custom-call(s32[1]{0:T(128)} %bitcast.1.place_ref, bf16[960,1280]{1,0:T(8,128)(2,1)} %get-tuple-element.65.turned_ref, f32[960,1]{1,0:T(8,128)} %broadcast_in_dim_tile.4.factor_ref, ...), custom_call_target="tpu_custom_call" | custom-call | flops 1887436800 | bytes 10485760 | tf_op jit(solution)/shard_map/pallas_call | solution.py:552
  136.9 1.5 collective-permute-start.14
  140.5 6.5 %collective-permute-start.17 = (bf16[320,384]{1,0:T(8,128)(2,1)}, bf16[320,384]{1,0:T(8,128)(2,1)}, u32[]{:S(2)}, u32[]{:S(2)}) collective-permute-start(bf16[320,384]{1,0:T(8,128)(2,1)} %get-tuple-element.166), channel_id=1, source_target_pairs={{0,2},{1,3},{2,0},{3,1},{4,6},{5,7},{6,4},{7,5},{8,10},{9,11},{10,... | collective-permute-start | bytes 737288 | tf_op jit(solution)/shard_map/ppermute | solution.py:701
  146.9 2.7 collective-permute-start.18
  150.2 5.5 %collective-permute-done.15.refs_7_ = bf16[240,768]{1,0:T(8,128)(2,1)} collective-permute-done((bf16[240,768]{1,0:T(8,128)(2,1)}, bf16[240,768]{1,0:T(8,128)(2,1)}, u32[]{:S(2)}, u32[]{:S(2)}) %collective-permute-start.15) | collective-permute-done | bytes 368672 | tf_op jit(solution)/shard_map/ppermute | solution.py:650
  155.7 31.0 %shard_map.172 = (f32[4,80,1536]{2,1,0:T(8,128)}, f32[4,1,1536]{2,1,0:T(1,128)}, bf16[4,240,1536]{2,1,0:T(8,128)(2,1)}, bf16[16,80,384]{2,1,0:T(8,128)(2,1)}) custom-call(s32[24]{0:T(128)} %convert_reduce_fusion.starts_ref, s32[1]{0:T(128)} %bitcast.1.place_ref, bf16[240,768]{1,0:T(8,128)(2,1)} %get-tuple-element.68.refs_0_, ...), custom_call_target="tpu_custom_call" | custom-call | flops 14495514624 | bytes 12582912 | tf_op jit(solution)/shard_map/pallas_call | solution.py:226
  186.7 9.4 %all-to-all-start = ((bf16[16,80,384]{2,1,0:T(8,128)(2,1)}), bf16[16,80,384]{2,1,0:T(8,128)(2,1)}, u32[]{:S(2)}, u32[]{:S(2)}) async-start(bf16[16,80,384]{2,1,0:T(8,128)(2,1)} %get-tuple-element.78), calls=%async_computation | async-start | bytes 1966080 | tf_op jit(solution)/shard_map/all_to_all | solution.py:799
  199.2 2.7 dynamic-slice_select_fusion.normed_ref
  201.9 1.9 collective-permute-done.22.refs_6_
  203.8 2.1 collective-permute-done.20.refs_3_
  205.9 10.5 %shard_map.173.w_hbm = bf16[3,1280,1280]{2,1,0:T(8,128)(2,1)} custom-call(s32[1]{0:T(128)} %bitcast.here_ref, s32[1]{0:T(128)} %bitcast.1.place_ref, s32[1]{0:T(128)} %bitcast.21.group_ref, bf16[4,176,960]{2,1,0:T(8,128)(2,1)} %copy-done.2, bf16[4,176,960]{2,1,0:T(8,128)(2,1)} %collective-permute-done.8.refs_1_, ...), custom_call_target="tpu_custom_call" | custom-call | bytes 20971520 | tf_op jit(solution)/shard_map/pallas_call | solution.py:455
  216.4 5.1 %all-to-all-done.att_ref = bf16[16,80,384]{2,1,0:T(8,128)(2,1)} async-done(((bf16[16,80,384]{2,1,0:T(8,128)(2,1)}), bf16[16,80,384]{2,1,0:T(8,128)(2,1)}, u32[]{:S(2)}, u32[]{:S(2)}) %all-to-all-start) | async-done | bytes 983072 | tf_op jit(solution)/shard_map/all_to_all | solution.py:799
  221.5 17.8 %shard_map.174 = (bf16[320,384]{1,0:T(8,128)(2,1)}, bf16[320,384]{1,0:T(8,128)(2,1)}, bf16[320,384]{1,0:T(8,128)(2,1)}, bf16[320,384]{1,0:T(8,128)(2,1)}, bf16[1...) custom-call(s32[1]{0:T(128)} %bitcast.here_ref, ...), custom_call_target="tpu_custom_call" | custom-call | flops 7549747200 | bytes 20971520 | tf_op jit(solution)/shard_map/pallas_call | solution.py:469
  239.4 3.7 all-to-all-start.1
  244.3 3.0 collective-permute-done.24.refs_2_
  247.3 10.2 %shard_map.175 = (bf16[4,160,960]{2,1,0:T(8,128)(2,1)}, bf16[4,160,960]{2,1,0:T(8,128)(2,1)}, bf16[4,160,960]{2,1,0:T(8,128)(2,1)}, bf16[4,160,960]{2,1,0:T(8,128)(2,1)}) custom-call(s32[1]{0:T(128)} %bitcast.here_ref, s32[1]{0:T(128)} %bitcast.21.group_ref, bf16[2,3,320,384]{3,2,1,0:T(8,128)(2,1)} %get-tuple-element.87.refs_0_, ...), custom_call_target="tpu_custom_call" | custom-call | flops 3774873600 | bytes 16777216 | tf_op jit(solution)/shard_map/pallas_call | solution.py:502
  257.5 6.9 %collective-permute-start.30 = (bf16[4,160,960]{2,1,0:T(8,128)(2,1)}, bf16[4,160,960]{2,1,0:T(8,128)(2,1)}, u32[]{:S(2)}, u32[]{:S(2)}) collective-permute-start(bf16[4,160,960]{2,1,0:T(8,128)(2,1)} %get-tuple-element.91), channel_id=1, source_target_pairs={{0,16},{4,20},{8,24},{12,28},{16,0},{20,4},{24,8},{28,12},{1,17},{... | collective-permute-start | bytes 3686408 | tf_op jit(solution)/shard_map/ppermute | solution.py:658
  265.8 2.7 all-to-all-done.1.go_ref
  269.5 45.1 %shard_map.176 = (bf16[240,1536]{1,0:T(8,128)(2,1)}, bf16[240,1536]{1,0:T(8,128)(2,1)}, bf16[240,1536]{1,0:T(8,128)(2,1)}, bf16[240,1536]{1,0:T(8,128)(2,1)}, f32[80,1]{1,0:T(8,128)}) custom-call(s32[24]{0:T(128)} %convert_reduce_fusion.starts_ref, s32[1]{0:T(128)} %bitcast.1.place_ref, f32[80,1]{1,0:T(8,128)} %copy.70.scale_ref, ...), custom_call_target="tpu_custom_call" | custom-call | flops 38654705664 | bytes 16777216 | tf_op jit(solution)/shard_map/pallas_call | solution.py:250
  314.7 2.4 collective-permute-done.29.refs_4_.refs_3_
  317.1 6.9 %collective-permute-done.31 = bf16[4,160,960]{2,1,0:T(8,128)(2,1)} collective-permute-done((bf16[4,160,960]{2,1,0:T(8,128)(2,1)}, bf16[4,160,960]{2,1,0:T(8,128)(2,1)}, u32[]{:S(2)}, u32[]{:S(2)}) %collective-permute-start.31) | collective-permute-done | bytes 1228832 | tf_op jit(solution)/shard_map/ppermute | solution.py:658
  324.0 3.3 add_convert_fusion
  328.1 2.4 collective-permute-start.34
  332.0 1.5 collective-permute-start.37
  333.5 6.5 %collective-permute-done.33 = bf16[160,960]{1,0:T(8,128)(2,1)S(1)} collective-permute-done((bf16[160,960]{1,0:T(8,128)(2,1)S(1)}, bf16[160,960]{1,0:T(8,128)(2,1)S(1)}, u32[]{:S(2)}, u32[]{:S(2)}) %collective-permute-start.33) | collective-permute-done | bytes 307232 | tf_op jit(solution)/shard_map/ppermute | solution.py:701
  340.0 12.6 %collective-permute-done.34 = bf16[160,960]{1,0:T(8,128)(2,1)S(1)} collective-permute-done((bf16[160,960]{1,0:T(8,128)(2,1)S(1)}, bf16[160,960]{1,0:T(8,128)(2,1)S(1)}, u32[]{:S(2)}, u32[]{:S(2)}) %collective-permute-start.34) | collective-permute-done | bytes 307232 | tf_op jit(solution)/shard_map/ppermute | solution.py:701
  352.8 9.8 %collective-permute-start.36 = (bf16[160,960]{1,0:T(8,128)(2,1)S(1)}, bf16[160,960]{1,0:T(8,128)(2,1)S(1)}, u32[]{:S(2)}, u32[]{:S(2)}) collective-permute-start(bf16[160,960]{1,0:T(8,128)(2,1)S(1)} %fusion.9), channel_id=1, source_target_pairs={{0,16},{16,0},{1,17},{17,1},{2,18},{18,2},{3,19},{19,3},{4,20},{20... | collective-permute-start | bytes 921608 | tf_op jit(solution)/shard_map/ppermute | solution.py:650
  362.6 5.6 %collective-permute-start.28 = (bf16[320,384]{1,0:T(8,128)(2,1)S(1)}, bf16[320,384]{1,0:T(8,128)(2,1)S(1)}, u32[]{:S(2)}, u32[]{:S(2)}) collective-permute-start(bf16[320,384]{1,0:T(8,128)(2,1)S(1)} %copy-done.24), channel_id=1, source_target_pairs={{0,3},{1,0},{2,1},{3,2},{4,7},{5,4},{6,5},{7,6},{8,11},{9,8},{10,9... | collective-permute-start | bytes 737288 | tf_op jit(solution)/shard_map/ppermute | solution.py:701
  368.2 2.7 collective-permute-start.27
  370.8 6.0 %collective-permute-start.26 = (bf16[320,384]{1,0:T(8,128)(2,1)S(1)}, bf16[320,384]{1,0:T(8,128)(2,1)S(1)}, u32[]{:S(2)}, u32[]{:S(2)}) collective-permute-start(bf16[320,384]{1,0:T(8,128)(2,1)S(1)} %copy-done.22), channel_id=1, source_target_pairs={{0,1},{1,2},{2,3},{3,0},{4,5},{5,6},{6,7},{7,4},{8,9},{9,10},{10,1... | collective-permute-start | bytes 737288 | tf_op jit(solution)/shard_map/ppermute | solution.py:701
  376.9 14.7 %collective-permute-done.27 = bf16[320,384]{1,0:T(8,128)(2,1)S(1)} collective-permute-done((bf16[320,384]{1,0:T(8,128)(2,1)S(1)}, bf16[320,384]{1,0:T(8,128)(2,1)S(1)}, u32[]{:S(2)}, u32[]{:S(2)}) %collective-permute-start.27) | collective-permute-done | bytes 245792 | tf_op jit(solution)/shard_map/ppermute | solution.py:701
  392.6 10.7 %shard_map.177 = bf16[4,336,1536]{2,1,0:T(8,128)(2,1)} custom-call(s32[1]{0:T(128)} %bitcast.here_ref, s32[1]{0:T(128)} %bitcast.1.place_ref, bf16[1280,960]{1,0:T(8,128)(2,1)} %get-tuple-element.115.whole_ref, bf16[1280,768]{1,0:T(8,128)(2,1)} %all-gather.3.cloned.1.call-done.normed_ref.refs_0_, ...), custom_call_target="tpu_custom_call" | custom-call | flops 3774873600 | bytes 16777216 | tf_op jit(solution)/shard_map/pallas_call | solution.py:600
  403.3 10.2 %shard_map.178 = (bf16[2,320,960]{2,1,0:T(8,128)(2,1)}, bf16[2,320,960]{2,1,0:T(8,128)(2,1)}, f32[1280,1]{1,0:T(8,128)}) custom-call(s32[1]{0:T(128)} %bitcast.1.place_ref, bf16[1280,960]{1,0:T(8,128)(2,1)} %get-tuple-element.115.whole_ref, bf16[1280,768]{1,0:T(8,128)(2,1)} %all-gather.3.cloned.1.call-done.normed_ref.refs_0_, ...), custom_call_target="tpu_custom_call" | custom-call | flops 3774873600 | bytes 12582912 | tf_op jit(solution)/shard_map/pallas_call | solution.py:631
  420.1 1.8 fusion.11
  422.8 2.8 collective-permute-done.40
  425.6 2.2 fusion.6
  429.5 6.4 %collective-permute-done.42 = f32[2640]{0:T(1024)S(1)} collective-permute-done((f32[2640]{0:T(1024)S(1)}, f32[2640]{0:T(1024)S(1)}, u32[]{:S(2)}, u32[]{:S(2)}) %collective-permute-start.42) | collective-permute-done | bytes 10592 | tf_op jit(solution)/shard_map/ppermute | solution.py:650
  438.9 2.7 collective-permute-done.43
  441.6 2.4 collective-permute-done.45
  444.0 1.8 fusion.4
  445.9 1.8 collective-permute-start.46
  449.5 11.4 %collective-permute-done.46 = bf16[320,960]{1,0:T(8,128)(2,1)S(1)} collective-permute-done((bf16[320,960]{1,0:T(8,128)(2,1)S(1)}, bf16[320,960]{1,0:T(8,128)(2,1)S(1)}, u32[]{:S(2)}, u32[]{:S(2)}) %collective-permute-start.46) | collective-permute-done | bytes 614432 | tf_op jit(solution)/shard_map/ppermute | solution.py:650
  462.2 1.8 copy.74
  465.2 3.0 copy.77
  468.2 8.1 %reduce-scatter.2.cloned.1.call-done = bf16[1,336,1536]{2,1,0:T(8,128)(2,1)} async-done(((bf16[4,336,1536]{2,1,0:T(8,128)(2,1)}), bf16[1,336,1536]{2,1,0:T(8,128)(2,1)}) %reduce-scatter.2.cloned.1.call-update) | async-done | bytes 1032208 | tf_op jit(solution)/shard_map/reduce_scatter | solution.py:862
  476.3 1.6 convert_element_type.156
  478.1 1.7 fusion.3
  (184 shorter events, 40.2 us)
Async XLA Ops:
  7.2 11.3 %copy-start = (f32[1536,320]{0,1:T(8,128)S(1)}, f32[1536,320]{0,1:T(8,128)}, u32[]{:S(2)}) copy-start(f32[1536,320]{0,1:T(8,128)} %param.10) | copy-start | bytes 5898244
  7.2 11.3 %copy-start.18 = (f32[320]{0:T(512)S(1)}, f32[320]{0:T(512)}, u32[]{:S(2)}) copy-start(f32[320]{0:T(512)} %param.12) | copy-start | bytes 3844
  7.2 85.7 %all-gather.3.cloned.1.call-start = ((), (), s32[]{:S(2)}) async-start(), calls=%async_computation.3 | async-start | bytes 2457600 | tf_op jit(solution)/shard_map/all_gather | solution.py:776
  9.1 4.7 collective-permute-start.3
  13.8 4.7 collective-permute-start.4
  19.7 111.5 %all-gather.5.cloned.1.call-start = ((), (), s32[]{:S(2)}) async-start(), calls=%async_computation.4 | async-start | bytes 2457600 | tf_op jit(solution)/shard_map/all_gather | solution.py:776
  22.7 14.8 %collective-permute-start.1 = (bf16[320,960]{1,0:T(8,128)(2,1)}, bf16[320,960]{1,0:T(8,128)(2,1)}, u32[]{:S(2)}, u32[]{:S(2)}) collective-permute-start(bf16[320,960]{1,0:T(8,128)(2,1)} %copy.64.refs_0_), channel_id=1, source_target_pairs={{0,8},{4,12},{8,0},{12,4},{1,9},{5,13},{9,1},{13,5},{2,10},{6,14},... | collective-permute-start | bytes 1843208 | tf_op jit(solution)/shard_map/ppermute | solution.py:650
  24.6 15.6 %collective-permute-start = (bf16[320,960]{1,0:T(8,128)(2,1)}, bf16[320,960]{1,0:T(8,128)(2,1)}, u32[]{:S(2)}, u32[]{:S(2)}) collective-permute-start(bf16[320,960]{1,0:T(8,128)(2,1)} %copy.64.refs_0_), channel_id=1, source_target_pairs={{0,4},{4,0},{8,12},{12,8},{1,5},{5,1},{9,13},{13,9},{2,6},{6,2},{1... | collective-permute-start | bytes 1843208 | tf_op jit(solution)/shard_map/ppermute | solution.py:650
  37.5 2.7 collective-permute-start.2
  46.4 45.5 %copy-start.25 = (f32[80]{0:T(128)S(1)}, f32[80]{0:T(128)}, u32[]{:S(2)}) copy-start(f32[80]{0:T(128)} %param.14) | copy-start | bytes 964
  46.5 33.6 %collective-permute-start.6 = (bf16[176,960]{1,0:T(8,128)(2,1)S(1)}, bf16[176,960]{1,0:T(8,128)(2,1)S(1)}, u32[]{:S(2)}, u32[]{:S(2)}) collective-permute-start(bf16[176,960]{1,0:T(8,128)(2,1)S(1)} %maximum_maximum_fusion), channel_id=1, source_target_pairs={{0,2},{1,3},{2,0},{3,1},{4,6},{5,7},{6,4},{7,5},{8,10},{9,11},{10,... | collective-permute-start | bytes 1013768 | tf_op jit(solution)/shard_map/ppermute | solution.py:701
  49.3 30.9 %collective-permute-start.7 = (bf16[176,960]{1,0:T(8,128)(2,1)S(1)}, bf16[176,960]{1,0:T(8,128)(2,1)S(1)}, u32[]{:S(2)}, u32[]{:S(2)}) collective-permute-start(bf16[176,960]{1,0:T(8,128)(2,1)S(1)} %maximum_maximum_fusion), channel_id=1, source_target_pairs={{0,3},{1,0},{2,1},{3,2},{4,7},{5,4},{6,5},{7,6},{8,11},{9,8},{10,9... | collective-permute-start | bytes 1013768 | tf_op jit(solution)/shard_map/ppermute | solution.py:701
  50.6 38.0 %collective-permute-start.5 = (bf16[176,960]{1,0:T(8,128)(2,1)S(1)}, bf16[176,960]{1,0:T(8,128)(2,1)S(1)}, u32[]{:S(2)}, u32[]{:S(2)}) collective-permute-start(bf16[176,960]{1,0:T(8,128)(2,1)S(1)} %maximum_maximum_fusion), channel_id=1, source_target_pairs={{0,1},{1,2},{2,3},{3,0},{4,5},{5,6},{6,7},{7,4},{8,9},{9,10},{10,1... | collective-permute-start | bytes 1013768 | tf_op jit(solution)/shard_map/ppermute | solution.py:701
  88.8 109.0 %copy-start.2 = (bf16[4,176,960]{2,1,0:T(8,128)(2,1)}, bf16[4,176,960]{2,1,0:T(8,128)(2,1)S(1)}, u32[]{:S(2)}) copy-start(bf16[4,176,960]{2,1,0:T(8,128)(2,1)S(1)} %pad_maximum_fusion.refs_0_) | copy-start | bytes 4055044
  88.8 48.1 %collective-permute-start.8 = (bf16[4,176,960]{2,1,0:T(8,128)(2,1)S(1)}, bf16[4,176,960]{2,1,0:T(8,128)(2,1)}, u32[]{:S(2)}, u32[]{:S(2)}) collective-permute-start(bf16[4,176,960]{2,1,0:T(8,128)(2,1)S(1)} %pad_maximum_fusion.refs_0_), channel_id=1, source_target_pairs={{0,16},{16,0},{1,17},{17,1},{2,18},{18,2},{3,19},{19,3},{4,20},{20... | collective-permute-start | bytes 4055048 | tf_op jit(solution)/shard_map/ppermute | solution.py:650
  90.4 46.5 %collective-permute-start.9 = (bf16[4,176,960]{2,1,0:T(8,128)(2,1)S(1)}, bf16[4,176,960]{2,1,0:T(8,128)(2,1)}, u32[]{:S(2)}, u32[]{:S(2)}) collective-permute-start(bf16[4,176,960]{2,1,0:T(8,128)(2,1)S(1)} %pad_maximum_fusion.refs_0_), channel_id=1, source_target_pairs={{0,8},{4,12},{8,0},{12,4},{1,9},{5,13},{9,1},{13,5},{2,10},{6,14},... | collective-permute-start | bytes 4055048 | tf_op jit(solution)/shard_map/ppermute | solution.py:650
  98.8 39.7 %collective-permute-start.10 = (bf16[240,768]{1,0:T(8,128)(2,1)}, bf16[240,768]{1,0:T(8,128)(2,1)}, u32[]{:S(2)}, u32[]{:S(2)}) collective-permute-start(bf16[240,768]{1,0:T(8,128)(2,1)} %get-tuple-element.69), channel_id=1, source_target_pairs={{0,4},{4,0},{8,12},{12,8},{1,5},{5,1},{9,13},{13,9},{2,6},{6,2},{1... | collective-permute-start | bytes 1105928 | tf_op jit(solution)/shard_map/ppermute | solution.py:650
  98.8 41.5 %collective-permute-start.11 = (bf16[240,768]{1,0:T(8,128)(2,1)}, bf16[240,768]{1,0:T(8,128)(2,1)}, u32[]{:S(2)}, u32[]{:S(2)}) collective-permute-start(bf16[240,768]{1,0:T(8,128)(2,1)} %get-tuple-element.70), channel_id=1, source_target_pairs={{0,8},{4,12},{8,0},{12,4},{1,9},{5,13},{9,1},{13,5},{2,10},{6,14},... | collective-permute-start | bytes 1105928 | tf_op jit(solution)/shard_map/ppermute | solution.py:650
  99.1 41.4 %collective-permute-start.12 = (bf16[240,768]{1,0:T(8,128)(2,1)}, bf16[240,768]{1,0:T(8,128)(2,1)}, u32[]{:S(2)}, u32[]{:S(2)}) collective-permute-start(bf16[240,768]{1,0:T(8,128)(2,1)} %get-tuple-element.71), channel_id=1, source_target_pairs={{0,12},{4,8},{8,4},{12,0},{1,13},{5,9},{9,5},{13,1},{2,14},{6,10},... | collective-permute-start | bytes 1105928 | tf_op jit(solution)/shard_map/ppermute | solution.py:650
  136.9 10.0 %collective-permute-start.13 = (bf16[240,768]{1,0:T(8,128)(2,1)}, bf16[240,768]{1,0:T(8,128)(2,1)}, u32[]{:S(2)}, u32[]{:S(2)}) collective-permute-start(bf16[240,768]{1,0:T(8,128)(2,1)} %get-tuple-element.74), channel_id=1, source_target_pairs={{0,4},{4,0},{8,12},{12,8},{1,5},{5,1},{9,13},{13,9},{2,6},{6,2},{1... | collective-permute-start | bytes 1105928 | tf_op jit(solution)/shard_map/ppermute | solution.py:650
  136.9 12.7 %collective-permute-start.14 = (bf16[240,768]{1,0:T(8,128)(2,1)}, bf16[240,768]{1,0:T(8,128)(2,1)}, u32[]{:S(2)}, u32[]{:S(2)}) collective-permute-start(bf16[240,768]{1,0:T(8,128)(2,1)} %get-tuple-element.75), channel_id=1, source_target_pairs={{0,8},{4,12},{8,0},{12,4},{1,9},{5,13},{9,1},{13,5},{2,10},{6,14},... | collective-permute-start | bytes 1105928 | tf_op jit(solution)/shard_map/ppermute | solution.py:650
  138.5 17.2 %collective-permute-start.15 = (bf16[240,768]{1,0:T(8,128)(2,1)}, bf16[240,768]{1,0:T(8,128)(2,1)}, u32[]{:S(2)}, u32[]{:S(2)}) collective-permute-start(bf16[240,768]{1,0:T(8,128)(2,1)} %get-tuple-element.76), channel_id=1, source_target_pairs={{0,12},{4,8},{8,4},{12,0},{1,13},{5,9},{9,5},{13,1},{2,14},{6,10},... | collective-permute-start | bytes 1105928 | tf_op jit(solution)/shard_map/ppermute | solution.py:650
  140.3 46.3 %collective-permute-start.16 = (bf16[320,384]{1,0:T(8,128)(2,1)}, bf16[320,384]{1,0:T(8,128)(2,1)}, u32[]{:S(2)}, u32[]{:S(2)}) collective-permute-start(bf16[320,384]{1,0:T(8,128)(2,1)} %get-tuple-element.167), channel_id=1, source_target_pairs={{0,1},{1,2},{2,3},{3,0},{4,5},{5,6},{6,7},{7,4},{8,9},{9,10},{10,1... | collective-permute-start | bytes 737288 | tf_op jit(solution)/shard_map/ppermute | solution.py:701
  140.5 46.2 %collective-permute-start.17 = (bf16[320,384]{1,0:T(8,128)(2,1)}, bf16[320,384]{1,0:T(8,128)(2,1)}, u32[]{:S(2)}, u32[]{:S(2)}) collective-permute-start(bf16[320,384]{1,0:T(8,128)(2,1)} %get-tuple-element.166), channel_id=1, source_target_pairs={{0,2},{1,3},{2,0},{3,1},{4,6},{5,7},{6,4},{7,5},{8,10},{9,11},{10,... | collective-permute-start | bytes 737288 | tf_op jit(solution)/shard_map/ppermute | solution.py:701
  146.9 39.7 %collective-permute-start.18 = (bf16[320,384]{1,0:T(8,128)(2,1)}, bf16[320,384]{1,0:T(8,128)(2,1)}, u32[]{:S(2)}, u32[]{:S(2)}) collective-permute-start(bf16[320,384]{1,0:T(8,128)(2,1)} %get-tuple-element.165), channel_id=1, source_target_pairs={{0,3},{1,0},{2,1},{3,2},{4,7},{5,4},{6,5},{7,6},{8,11},{9,8},{10,9... | collective-permute-start | bytes 737288 | tf_op jit(solution)/shard_map/ppermute | solution.py:701
  149.6 46.5 %collective-permute-start.21 = (bf16[4,176,960]{2,1,0:T(8,128)(2,1)}, bf16[4,176,960]{2,1,0:T(8,128)(2,1)}, u32[]{:S(2)}, u32[]{:S(2)}) collective-permute-start(bf16[4,176,960]{2,1,0:T(8,128)(2,1)} %collective-permute-done.9.refs_4_), channel_id=1, source_target_pairs={{0,16},{16,0},{1,17},{17,1},{2,18},{18,2},{3,19},{19,3},{4,20},{20... | collective-permute-start | bytes 4055048 | tf_op jit(solution)/shard_map/ppermute | solution.py:650
  186.7 34.9 %all-to-all-start = ((bf16[16,80,384]{2,1,0:T(8,128)(2,1)}), bf16[16,80,384]{2,1,0:T(8,128)(2,1)}, u32[]{:S(2)}, u32[]{:S(2)}) async-start(bf16[16,80,384]{2,1,0:T(8,128)(2,1)} %get-tuple-element.78), calls=%async_computation | async-start | bytes 1966080 | tf_op jit(solution)/shard_map/all_to_all | solution.py:799
  196.1 5.8 %collective-permute-start.23 = (bf16[4,176,960]{2,1,0:T(8,128)(2,1)}, bf16[4,176,960]{2,1,0:T(8,128)(2,1)}, u32[]{:S(2)}, u32[]{:S(2)}) collective-permute-start(bf16[4,176,960]{2,1,0:T(8,128)(2,1)} %collective-permute-done.21.refs_5_), channel_id=1, source_target_pairs={{0,4},{4,0},{8,12},{12,8},{1,5},{5,1},{9,13},{13,9},{2,6},{6,2},{1... | collective-permute-start | bytes 4055048 | tf_op jit(solution)/shard_map/ppermute | solution.py:650
  196.5 7.3 %collective-permute-start.22 = (bf16[4,176,960]{2,1,0:T(8,128)(2,1)}, bf16[4,176,960]{2,1,0:T(8,128)(2,1)}, u32[]{:S(2)}, u32[]{:S(2)}) collective-permute-start(bf16[4,176,960]{2,1,0:T(8,128)(2,1)} %collective-permute-done.9.refs_4_), channel_id=1, source_target_pairs={{0,4},{4,0},{8,12},{12,8},{1,5},{5,1},{9,13},{13,9},{2,6},{6,2},{1... | collective-permute-start | bytes 4055048 | tf_op jit(solution)/shard_map/ppermute | solution.py:650
  196.7 9.2 %collective-permute-start.20 = (bf16[4,176,960]{2,1,0:T(8,128)(2,1)}, bf16[4,176,960]{2,1,0:T(8,128)(2,1)}, u32[]{:S(2)}, u32[]{:S(2)}) collective-permute-start(bf16[4,176,960]{2,1,0:T(8,128)(2,1)} %collective-permute-done.8.refs_1_), channel_id=1, source_target_pairs={{0,4},{4,0},{8,12},{12,8},{1,5},{5,1},{9,13},{13,9},{2,6},{6,2},{1... | collective-permute-start | bytes 4055048 | tf_op jit(solution)/shard_map/ppermute | solution.py:650
  197.0 8.9 %collective-permute-start.19 = (bf16[4,176,960]{2,1,0:T(8,128)(2,1)S(1)}, bf16[4,176,960]{2,1,0:T(8,128)(2,1)}, u32[]{:S(2)}, u32[]{:S(2)}) collective-permute-start(bf16[4,176,960]{2,1,0:T(8,128)(2,1)S(1)} %pad_maximum_fusion.refs_0_), channel_id=1, source_target_pairs={{0,4},{4,0},{8,12},{12,8},{1,5},{5,1},{9,13},{13,9},{2,6},{6,2},{1... | collective-permute-start | bytes 4055048 | tf_op jit(solution)/shard_map/ppermute | solution.py:650
  239.3 8.0 %collective-permute-start.25 = (bf16[3,384,1280]{2,1,0:T(8,128)(2,1)}, bf16[3,384,1280]{2,1,0:T(8,128)(2,1)}, u32[]{:S(2)}, u32[]{:S(2)}) collective-permute-start(bf16[3,384,1280]{2,1,0:T(8,128)(2,1)} %get-tuple-element.88.refs_1_), channel_id=1, source_target_pairs={{0,4},{4,0},{8,12},{12,8},{1,5},{5,1},{9,13},{13,9},{2,6},{6,2},{1... | collective-permute-start | bytes 8847368 | tf_op jit(solution)/shard_map/ppermute | solution.py:650
  239.4 29.2 %all-to-all-start.1 = ((bf16[16,80,384]{2,1,0:T(8,128)(2,1)}), bf16[16,80,384]{2,1,0:T(8,128)(2,1)S(1)}, u32[]{:S(2)}, u32[]{:S(2)}) async-start(bf16[16,80,384]{2,1,0:T(8,128)(2,1)} %get-tuple-element.86), calls=%async_computation.1 | async-start | bytes 1966080 | tf_op jit(solution)/shard_map/all_to_all | solution.py:829
  243.1 233.2 %reduce-scatter.2.cloned.1.call-start = ((), (), s32[]{:S(2)}) async-start(), calls=%async_computation.5 | async-start | bytes 5160960 | tf_op jit(solution)/shard_map/reduce_scatter | solution.py:862
  243.1 4.2 collective-permute-start.24
  257.5 59.6 %collective-permute-start.30 = (bf16[4,160,960]{2,1,0:T(8,128)(2,1)}, bf16[4,160,960]{2,1,0:T(8,128)(2,1)}, u32[]{:S(2)}, u32[]{:S(2)}) collective-permute-start(bf16[4,160,960]{2,1,0:T(8,128)(2,1)} %get-tuple-element.91), channel_id=1, source_target_pairs={{0,16},{4,20},{8,24},{12,28},{16,0},{20,4},{24,8},{28,12},{1,17},{... | collective-permute-start | bytes 3686408 | tf_op jit(solution)/shard_map/ppermute | solution.py:658
  264.4 59.6 %collective-permute-start.31 = (bf16[4,160,960]{2,1,0:T(8,128)(2,1)}, bf16[4,160,960]{2,1,0:T(8,128)(2,1)}, u32[]{:S(2)}, u32[]{:S(2)}) collective-permute-start(bf16[4,160,960]{2,1,0:T(8,128)(2,1)} %get-tuple-element.92), channel_id=1, source_target_pairs={{0,8},{4,12},{8,0},{12,4},{16,24},{20,28},{24,16},{28,20},{1,9},{5... | collective-permute-start | bytes 3686408 | tf_op jit(solution)/shard_map/ppermute | solution.py:658
  265.7 58.3 %collective-permute-start.32 = (bf16[4,160,960]{2,1,0:T(8,128)(2,1)}, bf16[4,160,960]{2,1,0:T(8,128)(2,1)}, u32[]{:S(2)}, u32[]{:S(2)}) collective-permute-start(bf16[4,160,960]{2,1,0:T(8,128)(2,1)} %get-tuple-element.93), channel_id=1, source_target_pairs={{0,24},{4,28},{8,16},{12,20},{16,8},{20,12},{24,0},{28,4},{1,25},{... | collective-permute-start | bytes 3686408 | tf_op jit(solution)/shard_map/ppermute | solution.py:658
  269.5 54.5 %copy-start.4 = (bf16[4,160,960]{2,1,0:T(8,128)(2,1)S(1)}, bf16[4,160,960]{2,1,0:T(8,128)(2,1)}, u32[]{:S(2)}) copy-start(bf16[4,160,960]{2,1,0:T(8,128)(2,1)} %get-tuple-element.108) | copy-start | bytes 3686404
  314.7 2.4 collective-permute-start.29
  317.1 10.2 %copy-start.6 = (bf16[240,1536]{1,0:T(8,128)(2,1)}, bf16[240,1536]{1,0:T(8,128)(2,1)S(1)}, u32[]{:S(2)}) copy-start(bf16[240,1536]{1,0:T(8,128)(2,1)S(1)} %collective-permute-done.29.refs_4_.refs_3_) | copy-start | bytes 2211844
  327.3 35.3 %copy-start.24 = (bf16[320,384]{1,0:T(8,128)(2,1)S(1)}, bf16[320,384]{1,0:T(8,128)(2,1)}, u32[]{:S(2)}) copy-start(bf16[320,384]{1,0:T(8,128)(2,1)} %get-tuple-element.101) | copy-start | bytes 737284
  327.3 40.9 %copy-start.23 = (bf16[320,384]{1,0:T(8,128)(2,1)S(1)}, bf16[320,384]{1,0:T(8,128)(2,1)}, u32[]{:S(2)}) copy-start(bf16[320,384]{1,0:T(8,128)(2,1)} %get-tuple-element.99) | copy-start | bytes 737284
  327.3 43.5 %copy-start.22 = (bf16[320,384]{1,0:T(8,128)(2,1)S(1)}, bf16[320,384]{1,0:T(8,128)(2,1)}, u32[]{:S(2)}) copy-start(bf16[320,384]{1,0:T(8,128)(2,1)} %get-tuple-element.97) | copy-start | bytes 737284
  327.4 12.6 %collective-permute-start.33 = (bf16[160,960]{1,0:T(8,128)(2,1)S(1)}, bf16[160,960]{1,0:T(8,128)(2,1)S(1)}, u32[]{:S(2)}, u32[]{:S(2)}) collective-permute-start(bf16[160,960]{1,0:T(8,128)(2,1)S(1)} %get-tuple-element.162), channel_id=1, source_target_pairs={{0,1},{1,2},{2,3},{3,0},{4,5},{5,6},{6,7},{7,4},{8,9},{9,10},{10,1... | collective-permute-start | bytes 921608 | tf_op jit(solution)/shard_map/ppermute | solution.py:701
  328.1 24.4 %collective-permute-start.34 = (bf16[160,960]{1,0:T(8,128)(2,1)S(1)}, bf16[160,960]{1,0:T(8,128)(2,1)S(1)}, u32[]{:S(2)}, u32[]{:S(2)}) collective-permute-start(bf16[160,960]{1,0:T(8,128)(2,1)S(1)} %get-tuple-element.164), channel_id=1, source_target_pairs={{0,2},{1,3},{2,0},{3,1},{4,6},{5,7},{6,4},{7,5},{8,10},{9,11},{10,... | collective-permute-start | bytes 921608 | tf_op jit(solution)/shard_map/ppermute | solution.py:701
  330.5 22.1 %collective-permute-start.35 = (bf16[160,960]{1,0:T(8,128)(2,1)S(1)}, bf16[160,960]{1,0:T(8,128)(2,1)S(1)}, u32[]{:S(2)}, u32[]{:S(2)}) collective-permute-start(bf16[160,960]{1,0:T(8,128)(2,1)S(1)} %get-tuple-element.163), channel_id=1, source_target_pairs={{0,3},{1,0},{2,1},{3,2},{4,7},{5,4},{6,5},{7,6},{8,11},{9,8},{10,9... | collective-permute-start | bytes 921608 | tf_op jit(solution)/shard_map/ppermute | solution.py:701
  332.0 59.7 %collective-permute-start.37 = (bf16[240,1536]{1,0:T(8,128)(2,1)S(1)}, bf16[240,1536]{1,0:T(8,128)(2,1)S(1)}, u32[]{:S(2)}, u32[]{:S(2)}) collective-permute-start(bf16[240,1536]{1,0:T(8,128)(2,1)S(1)} %copy-done.21), channel_id=1, source_target_pairs={{0,8},{4,12},{8,0},{12,4},{1,9},{5,13},{9,1},{13,5},{2,10},{6,14},... | collective-permute-start | bytes 2211848 | tf_op jit(solution)/shard_map/ppermute | solution.py:650
  333.5 58.2 %collective-permute-start.38 = (bf16[240,1536]{1,0:T(8,128)(2,1)S(1)}, bf16[240,1536]{1,0:T(8,128)(2,1)}, u32[]{:S(2)}, u32[]{:S(2)}) collective-permute-start(bf16[240,1536]{1,0:T(8,128)(2,1)S(1)} %copy-done.20), channel_id=1, source_target_pairs={{0,12},{4,8},{8,4},{12,0},{1,13},{5,9},{9,5},{13,1},{2,14},{6,10},... | collective-permute-start | bytes 2211848 | tf_op jit(solution)/shard_map/ppermute | solution.py:650
  352.8 18.0 %collective-permute-start.36 = (bf16[160,960]{1,0:T(8,128)(2,1)S(1)}, bf16[160,960]{1,0:T(8,128)(2,1)S(1)}, u32[]{:S(2)}, u32[]{:S(2)}) collective-permute-start(bf16[160,960]{1,0:T(8,128)(2,1)S(1)} %fusion.9), channel_id=1, source_target_pairs={{0,16},{16,0},{1,17},{17,1},{2,18},{18,2},{3,19},{19,3},{4,20},{20... | collective-permute-start | bytes 921608 | tf_op jit(solution)/shard_map/ppermute | solution.py:650
  362.6 14.3 %collective-permute-start.28 = (bf16[320,384]{1,0:T(8,128)(2,1)S(1)}, bf16[320,384]{1,0:T(8,128)(2,1)S(1)}, u32[]{:S(2)}, u32[]{:S(2)}) collective-permute-start(bf16[320,384]{1,0:T(8,128)(2,1)S(1)} %copy-done.24), channel_id=1, source_target_pairs={{0,3},{1,0},{2,1},{3,2},{4,7},{5,4},{6,5},{7,6},{8,11},{9,8},{10,9... | collective-permute-start | bytes 737288 | tf_op jit(solution)/shard_map/ppermute | solution.py:701
  368.2 23.4 %collective-permute-start.27 = (bf16[320,384]{1,0:T(8,128)(2,1)S(1)}, bf16[320,384]{1,0:T(8,128)(2,1)S(1)}, u32[]{:S(2)}, u32[]{:S(2)}) collective-permute-start(bf16[320,384]{1,0:T(8,128)(2,1)S(1)} %copy-done.23), channel_id=1, source_target_pairs={{0,2},{1,3},{2,0},{3,1},{4,6},{5,7},{6,4},{7,5},{8,10},{9,11},{10,... | collective-permute-start | bytes 737288 | tf_op jit(solution)/shard_map/ppermute | solution.py:701
  370.8 20.8 %collective-permute-start.26 = (bf16[320,384]{1,0:T(8,128)(2,1)S(1)}, bf16[320,384]{1,0:T(8,128)(2,1)S(1)}, u32[]{:S(2)}, u32[]{:S(2)}) collective-permute-start(bf16[320,384]{1,0:T(8,128)(2,1)S(1)} %copy-done.22), channel_id=1, source_target_pairs={{0,1},{1,2},{2,3},{3,0},{4,5},{5,6},{6,7},{7,4},{8,9},{9,10},{10,1... | collective-permute-start | bytes 737288 | tf_op jit(solution)/shard_map/ppermute | solution.py:701
  376.9 14.7 %copy-start.13 = (bf16[320,384]{1,0:T(8,128)(2,1)}, bf16[320,384]{1,0:T(8,128)(2,1)S(1)}, u32[]{:S(2)}) copy-start(bf16[320,384]{1,0:T(8,128)(2,1)S(1)} %collective-permute-done.28) | copy-start | bytes 737284
  403.3 10.3 %copy-start.8 = (f32[1280,1]{1,0:T(8,128)S(1)}, f32[1280,1]{1,0:T(8,128)}, u32[]{:S(2)}) copy-start(f32[1280,1]{1,0:T(8,128)} %get-tuple-element.117) | copy-start | bytes 15364
  413.6 12.0 %collective-permute-start.44 = (bf16[2,320,960]{2,1,0:T(8,128)(2,1)}, bf16[2,320,960]{2,1,0:T(8,128)(2,1)}, u32[]{:S(2)}, u32[]{:S(2)}) collective-permute-start(bf16[2,320,960]{2,1,0:T(8,128)(2,1)} %get-tuple-element.120), channel_id=1, source_target_pairs={{0,4},{4,0},{8,12},{12,8},{1,5},{5,1},{9,13},{13,9},{2,6},{6,2},{1... | collective-permute-start | bytes 3686408 | tf_op jit(solution)/shard_map/ppermute | solution.py:650
  419.5 2.4 collective-permute-start.39
  421.9 3.7 collective-permute-start.40
  425.6 3.7 collective-permute-start.41
  427.8 16.2 %collective-permute-start.45 = (bf16[320,960]{1,0:T(8,128)(2,1)}, bf16[320,960]{1,0:T(8,128)(2,1)}, u32[]{:S(2)}, u32[]{:S(2)}) collective-permute-start(bf16[320,960]{1,0:T(8,128)(2,1)} %fusion.6), channel_id=1, source_target_pairs={{0,8},{4,12},{8,0},{12,4},{1,9},{5,13},{9,1},{13,5},{2,10},{6,14},... | collective-permute-start | bytes 1843208 | tf_op jit(solution)/shard_map/ppermute | solution.py:650
  429.3 6.6 %collective-permute-start.42 = (f32[2640]{0:T(1024)S(1)}, f32[2640]{0:T(1024)S(1)}, u32[]{:S(2)}, u32[]{:S(2)}) collective-permute-start(f32[2640]{0:T(1024)S(1)} %add.197), channel_id=1, source_target_pairs={{0,1},{1,0},{2,3},{3,2},{4,5},{5,4},{6,7},{7,6},{8,9},{9,8},{10,11... | collective-permute-start | bytes 31688 | tf_op jit(solution)/shard_map/ppermute | solution.py:650
  436.0 5.7 %collective-permute-start.43 = (f32[2640]{0:T(1024)S(1)}, f32[2640]{0:T(1024)S(1)}, u32[]{:S(2)}, u32[]{:S(2)}) collective-permute-start(f32[2640]{0:T(1024)S(1)} %add.198), channel_id=1, source_target_pairs={{0,2},{1,3},{2,0},{3,1},{4,6},{5,7},{6,4},{7,5},{8,10},{9,11},{10,... | collective-permute-start | bytes 31688 | tf_op jit(solution)/shard_map/ppermute | solution.py:650
  437.9 11.0 %copy-start.26 = (f32[80]{0:T(128)S(1)}, f32[80]{0:T(128)}, u32[]{:S(2)}) copy-start(f32[80]{0:T(128)} %param.14) | copy-start | bytes 964
  445.9 15.1 %collective-permute-start.46 = (bf16[320,960]{1,0:T(8,128)(2,1)S(1)}, bf16[320,960]{1,0:T(8,128)(2,1)S(1)}, u32[]{:S(2)}, u32[]{:S(2)}) collective-permute-start(bf16[320,960]{1,0:T(8,128)(2,1)S(1)} %fusion.4), channel_id=1, source_target_pairs={{0,16},{16,0},{1,17},{17,1},{2,18},{18,2},{3,19},{19,3},{4,20},{20... | collective-permute-start | bytes 1843208 | tf_op jit(solution)/shard_map/ppermute | solution.py:650
  (15 other events, 46.5 us)
Sparse Core Ops, SparseCore 0:
  19.9 60.1 all-gather.2
  82.2 48.9 all-gather.4
  403.5 72.7 reduce-scatter.1
